TPU v7x, 256 devices: a whole 4x4x8 slice. The times are simulated.
256 devices in a mesh: row: 4 (over z_lo, core), col: 16 (over x, y), chan: 4 (over z_hi).
Axes of the slice: x: 4, y: 4, z: 8 (z_hi: 4, z_lo: 2; z = z_hi * 2 + z_lo), core: 2. Of those that a mesh axis runs over, the one named last changes fastest.
Arguments:
- pair: bfloat16 [1024, 1024, 128], P('row', 'col'), may hold values from -6 to 6
- pair_mask: int32 [1024, 1024], P('row', 'col'), may hold values 0 or 1
- ln_gain: float32 [128], replicated, may hold values from 0.1 to 1.9
- ln_bias: float32 [128], replicated, may hold values from -3 to 3
- left_value: bfloat16 [128, 128], P(None, 'chan'), may hold values from -0.5 to 0.5
- left_gate: bfloat16 [128, 128], P(None, 'chan'), may hold values from -0.5 to 0.5
- right_value: bfloat16 [128, 128], P(None, 'chan'), may hold values from -0.5 to 0.5
- right_gate: bfloat16 [128, 128], P(None, 'chan'), may hold values from -0.5 to 0.5
- hid_gain: float32 [128], replicated, may hold values from 0.1 to 1.9
- hid_bias: float32 [128], replicated, may hold values from -3 to 3
- out_weight: bfloat16 [128, 128], replicated, may hold values from -0.5 to 0.5
- out_gate: bfloat16 [128, 128], replicated, may hold values from -0.5 to 0.5
Outputs:
- update: bfloat16 [1024, 1024, 128], P('row', ('col', 'chan'))
All inputs are finite; a program needn't handle non-finite values. No bound on the sum of `pair_mask` on one device may be relied on, other than what follows from the above.
Results may differ from a plain program's by a relative error of at most 0.025.
Values may be sent and summed in bfloat16 or wider, within the bound.
No kernel may reach another device: no remote copies, remote signals or barrier semaphores. Data moves between devices by JAX's collectives and lax.ppermute only.
A program may use at most 128 MiB of HBM per device.

v0:
```python
import jax
import jax.numpy as jnp
from jax import lax
from jax.sharding import PartitionSpec as P


def on_device(
    pair,
    pair_mask,
    ln_gain,
    ln_bias,
    left_value,
    left_gate,
    right_value,
    right_gate,
    hid_gain,
    hid_bias,
    out_weight,
    out_gate,
):
    tile_cols = pair.shape[1]
    group_width = left_value.shape[1]
    out_cols = tile_cols // lax.axis_size("chan")
    group_index = lax.axis_index("chan")
    source = pair.astype(jnp.float32)
    centre = jnp.mean(source, axis=-1, keepdims=True)
    shifted = source - centre
    spread = jnp.mean(shifted * shifted, axis=-1, keepdims=True)
    normed = (shifted * lax.rsqrt(spread + 1e-05) * ln_gain + ln_bias).astype(jnp.bfloat16)
    weights = jnp.concatenate([left_value, left_gate, right_value, right_gate], axis=1)
    projected_all = jnp.einsum("ikc,cq->qik", normed, weights, preferred_element_type=jnp.float32)
    valid = pair_mask.astype(jnp.float32)[None, :, :]
    left = (
        jax.nn.sigmoid(projected_all[group_width : 2 * group_width])
        * projected_all[:group_width]
        * valid
    ).astype(jnp.bfloat16)
    right = (
        jax.nn.sigmoid(projected_all[3 * group_width :])
        * projected_all[2 * group_width : 3 * group_width]
        * valid
    ).astype(jnp.bfloat16)
    own_normed = lax.dynamic_slice_in_dim(normed, group_index * out_cols, out_cols, 1)
    gating = jax.nn.sigmoid(
        jnp.einsum("ijc,cd->ijd", own_normed, out_gate, preferred_element_type=jnp.float32)
    )
    right_all = lax.all_gather(right, "row", axis=1, tiled=True)
    product = lax.psum_scatter(
        jnp.einsum("hik,hjk->jhi", left, right_all, preferred_element_type=jnp.float32).astype(
            jnp.bfloat16
        ),
        "col",
        scatter_dimension=0,
        tiled=True,
    ).astype(jnp.float32)
    product = product.astype(jnp.bfloat16)
    widened = product.astype(jnp.float32)
    first_sums = jnp.sum(widened, axis=1)
    second_sums = jnp.sum(widened * widened, axis=1)
    first_sums, second_sums = (
        lax.psum(first_sums.astype(jnp.bfloat16), "chan").astype(jnp.float32),
        lax.psum(second_sums.astype(jnp.bfloat16), "chan").astype(jnp.float32),
    )
    total_width = group_width * lax.axis_size("chan")
    mean_hid = first_sums / total_width
    spread_hid = second_sums / total_width - mean_hid * mean_hid
    gain_part = lax.dynamic_slice_in_dim(hid_gain, group_index * group_width, group_width, 0)
    bias_part = lax.dynamic_slice_in_dim(hid_bias, group_index * group_width, group_width, 0)
    weight_rows = lax.dynamic_slice_in_dim(out_weight, group_index * group_width, group_width, 0)
    hidden = (
        (widened - mean_hid[:, None, :])
        * lax.rsqrt(spread_hid + 1e-05)[:, None, :]
        * gain_part[None, :, None]
        + bias_part[None, :, None]
    ).astype(jnp.bfloat16)
    mixed = lax.psum_scatter(
        jnp.einsum("jhi,hd->jid", hidden, weight_rows, preferred_element_type=jnp.float32).astype(
            jnp.bfloat16
        ),
        "chan",
        scatter_dimension=0,
        tiled=True,
    ).astype(jnp.float32)
    return (gating * jnp.transpose(mixed, (1, 0, 2))).astype(jnp.bfloat16)


def solution(mesh):
    return jax.shard_map(
        on_device,
        mesh=mesh,
        in_specs=(
            P("row", "col", None),
            P("row", "col"),
            P(),
            P(),
            P(None, "chan"),
            P(None, "chan"),
            P(None, "chan"),
            P(None, "chan"),
            P(),
            P(),
            P(),
            P(),
        ),
        out_specs=P("row", ("col", "chan"), None),
        check_vma=False,
    )
```

profile of v0, /device:TPU:1, one launch (start us, length us, event | category | flops | bytes accessed | tf_op | source)
XLA Modules:
  0.0 375.0 jit_solution(5184248092818221821)
XLA Ops:
  6.5 0.0 all-gather.2.cloned.1.call-start
  6.6 10.7 %convert_reduce_fusion = f32[256,64]{0,1:T(8,128)S(1)} fusion(bf16[256,64,128]{2,1,0:T(8,128)(2,1)} %param.12), kind=kLoop, calls=%fused_computation.2 | loop fusion | flops 4177920 | bytes 4259840 | tf_op jit(solution)/shard_map/reduce_sum | solution.py:26
  17.3 11.6 %fusion.2 = f32[256,64]{0,1:T(8,128)S(1)} fusion(f32[256,64]{0,1:T(8,128)S(1)} %broadcast_multiply_fusion, bf16[256,64,128]{2,1,0:T(8,128)(2,1)S(1)} %copy-done.1), kind=kLoop, calls=%fused_computation.5 | loop fusion | flops 8372224 | bytes 4325376 | tf_op jit(solution)/shard_map/reduce_sum | solution.py:28
  29.0 0.0 copy-start.4
  29.0 0.0 copy-start.5
  29.0 0.0 copy-start.6
  29.1 9.3 %fusion.5 = bf16[256,64,128]{2,0,1:T(8,128)(2,1)S(1)} fusion(f32[128]{0:T(128)S(1)} %copy-done.8, f32[128]{0:T(128)S(1)} %copy-done.9, f32[256,64]{0,1:T(8,128)S(1)} %add_rsqrt_fusion.1, f32[256,64]{0,1:T(8,128)S(1)} %broadcast_multiply_fusion, bf16[256,64,128]{2,1,0:T(8,128)(2,1)S(1)} %copy-done.1), kind=kLoop, calls=%fused_computation.8 | loop fusion | flops 12582912 | bytes 8520704 | tf_op jit(solution)/shard_map/convert_element_type | solution.py:29
  38.4 1.3 fusion.26
  39.7 0.7 copy-done.2
  40.3 2.4 fusion.13
  42.7 0.0 all-gather.2.cloned.1.call-update
  42.8 0.0 reduce-scatter.3.cloned.1.call-start
  42.8 53.4 %all-gather.2.cloned.1.call-done = bf16[32,1024,64]{1,0,2:T(8,128)(2,1)} async-done(((bf16[32,256,64]{1,0,2:T(8,128)(2,1)}), bf16[32,1024,64]{1,0,2:T(8,128)(2,1)}) %all-gather.2.cloned.1.call-update) | async-done | bytes 4194320 | tf_op jit(solution)/shard_map/all_gather | solution.py:47
  96.2 10.3 %convert_bitcast_fusion = bf16[1024,32,256]{2,0,1:T(8,128)(2,1)} fusion(bf16[32,1024,64]{1,0,2:T(8,128)(2,1)} %all-gather.2.cloned.1.call-done, bf16[32,256,64]{1,0,2:T(8,128)(2,1)S(1)} %get-tuple-element.7), kind=kOutput, calls=%fused_computation | convolution fusion | flops 1082130432 | bytes 22020096 | tf_op jit(solution)/shard_map/hik,hjk->jhi/dot_general | solution.py:49
  106.5 0.0 reduce-scatter.3.cloned.1.call-update
  106.5 0.0 all-reduce.3.cloned.1.call-start
  106.6 115.2 %reduce-scatter.3.cloned.1.call-done = bf16[64,32,256]{2,0,1:T(8,128)(2,1)} async-done(((bf16[1024,32,256]{2,0,1:T(8,128)(2,1)}), bf16[64,32,256]{2,0,1:T(8,128)(2,1)}) %reduce-scatter.3.cloned.1.call-update) | async-done | bytes 1048592 | tf_op jit(solution)/shard_map/reduce_scatter | solution.py:48
  221.8 2.1 fusion.11
  223.8 2.0 reduce_sum.41
  225.8 0.0 all-reduce.3.cloned.1.call-update
  225.8 0.3 reduce-scatter.5.cloned.1.call-start
  226.1 0.1 dynamic_slice.13
  226.2 0.1 dynamic_slice.14
  226.3 47.2 %all-reduce.3.cloned.1.call-done = (bf16[64,256]{1,0:T(8,128)(2,1)}, bf16[64,256]{1,0:T(8,128)(2,1)}) async-done(((bf16[64,256]{1,0:T(8,128)(2,1)}, bf16[64,256]{1,0:T(8,128)(2,1)}), (bf16[64,256]{1,0:T(8,128)(2,1)}, bf16[64,256]{1,0:T(8,128)(2,1)})) %all-reduce.3.cloned.1.call-update) | async-done | bytes 65552 | tf_op jit(solution)/shard_map/psum | solution.py:62
  273.5 0.8 convert_multiply_fusion.1
  274.3 1.6 fusion.10
  275.9 0.0 copy-start.10
  275.9 3.3 convolution_convert_fusion
  279.2 0.0 reduce-scatter.5.cloned.1.call-update
  279.2 85.3 %reduce-scatter.5.cloned.1.call-done = bf16[16,256,128]{2,1,0:T(8,128)(2,1)} async-done(((bf16[64,256,128]{2,1,0:T(8,128)(2,1)}), bf16[16,256,128]{2,1,0:T(8,128)(2,1)}) %reduce-scatter.5.cloned.1.call-update) | async-done | bytes 1048592 | tf_op jit(solution)/shard_map/reduce_scatter | solution.py:76
  364.5 2.2 fusion.22
  366.8 1.6 copy.17
  (24 shorter events, 0.1 us)
Async XLA Ops:
  6.5 269.4 %copy-start = (bf16[128,128]{1,0:T(8,128)(2,1)S(1)}, bf16[128,128]{1,0:T(8,128)(2,1)}, u32[]{:S(2)}) copy-start(bf16[128,128]{1,0:T(8,128)(2,1)} %param.22) | copy-start | bytes 98308
  6.5 22.4 %copy-start.3 = (s32[256,64]{0,1:T(8,128)S(1)}, s32[256,64]{0,1:T(8,128)}, u32[]{:S(2)}) copy-start(s32[256,64]{0,1:T(8,128)} %param.13) | copy-start | bytes 196612
  6.5 22.5 %copy-start.9 = (f32[128]{0:T(128)S(1)}, f32[128]{0:T(128)}, u32[]{:S(2)}) copy-start(f32[128]{0:T(128)} %param.14) | copy-start | bytes 1540
  6.5 22.5 %copy-start.8 = (f32[128]{0:T(128)S(1)}, f32[128]{0:T(128)}, u32[]{:S(2)}) copy-start(f32[128]{0:T(128)} %param.15) | copy-start | bytes 1540
  6.5 89.7 %all-gather.2.cloned.1.call-start = ((), (), s32[]{:S(2)}) async-start(), calls=%async_computation.2 | async-start | bytes 5242880 | tf_op jit(solution)/shard_map/all_gather | solution.py:47
  6.6 10.7 %copy-start.1 = (bf16[256,64,128]{2,1,0:T(8,128)(2,1)S(1)}, bf16[256,64,128]{2,1,0:T(8,128)(2,1)}, u32[]{:S(2)}) copy-start(bf16[256,64,128]{2,1,0:T(8,128)(2,1)} %param.12) | copy-start | bytes 12582916
  29.0 9.3 %copy-start.4 = (bf16[128,32]{0,1:T(8,128)(2,1)S(1)}, bf16[128,32]{0,1:T(8,128)(2,1)}, u32[]{:S(2)}) copy-start(bf16[128,32]{0,1:T(8,128)(2,1)} %param.19) | copy-start | bytes 24580
  29.0 9.3 %copy-start.5 = (bf16[128,32]{0,1:T(8,128)(2,1)S(1)}, bf16[128,32]{0,1:T(8,128)(2,1)}, u32[]{:S(2)}) copy-start(bf16[128,32]{0,1:T(8,128)(2,1)} %param.18) | copy-start | bytes 24580
  29.0 9.3 %copy-start.6 = (bf16[128,32]{0,1:T(8,128)(2,1)S(1)}, bf16[128,32]{0,1:T(8,128)(2,1)}, u32[]{:S(2)}) copy-start(bf16[128,32]{0,1:T(8,128)(2,1)} %param.17) | copy-start | bytes 24580
  29.1 9.3 %copy-start.7 = (bf16[128,32]{0,1:T(8,128)(2,1)S(1)}, bf16[128,32]{0,1:T(8,128)(2,1)}, u32[]{:S(2)}) copy-start(bf16[128,32]{0,1:T(8,128)(2,1)} %param.16) | copy-start | bytes 24580
  38.4 1.9 copy-start.2
  42.8 179.0 %reduce-scatter.3.cloned.1.call-start = ((), (), s32[]{:S(2)}) async-start(), calls=%async_computation.3 | async-start | bytes 17825792 | tf_op jit(solution)/shard_map/reduce_scatter | solution.py:48
  106.5 119.6 %copy-start.11 = (f32[128]{0:T(128)S(1)}, f32[128]{0:T(128)}, u32[]{:S(2)}) copy-start(f32[128]{0:T(128)} %param.20) | copy-start | bytes 1540
  106.5 119.7 %copy-start.12 = (f32[128]{0:T(128)S(1)}, f32[128]{0:T(128)}, u32[]{:S(2)}) copy-start(f32[128]{0:T(128)} %param.21) | copy-start | bytes 1540
  106.5 167.0 %all-reduce.3.cloned.1.call-start = ((), (), s32[]{:S(2)}) async-start(), calls=%async_computation.5 | async-start | bytes 131072 | tf_op jit(solution)/shard_map/psum | solution.py:62
  225.8 138.7 %reduce-scatter.5.cloned.1.call-start = ((), (), s32[]{:S(2)}) async-start(), calls=%async_computation.4 | async-start | bytes 5242880 | tf_op jit(solution)/shard_map/reduce_scatter | solution.py:76
  275.9 88.6 %copy-start.10 = (bf16[128,128]{1,0:T(8,128)(2,1)S(1)}, bf16[128,128]{1,0:T(8,128)(2,1)}, u32[]{:S(2)}) copy-start(bf16[128,128]{1,0:T(8,128)(2,1)} %param.23) | copy-start | bytes 98308
Sparse Core Ops, SparseCore 0:
  42.9 53.2 all-gather.1
  106.6 115.0 reduce-scatter.2
  226.0 47.4 all-reduce.2
  279.4 85.1 reduce-scatter.4
where the time goes:
time: 375 us
  waiting for transfers between devices  301 us (80%)
  other arithmetic  40.5 us (11%)
  matrix products  17 us (5%)
  between operations  13.3 us (4%)
    reduce_scatter x1, waiting for transfers between devices, on_device(): lax.psum_scatter(jnp.einsum('hik,hjk->jhi', left, right_all, preferred_el...  115 us
    reduce_scatter x1, waiting for transfers between devices, on_device(): lax.psum_scatter(jnp.einsum('jhi,hd->jid', hidden, weight_rows, preferred...  85.3 us
    all_gather x1, waiting for transfers between devices, on_device(): right_all = lax.all_gather(right, 'row', axis=1, tiled=True)  53.4 us
    psum x1, waiting for transfers between devices, on_device(): lax.psum(second_sums.astype(jnp.bfloat16), 'chan').astype(jnp.float32)  47.2 us
    reduce_sum x1, other arithmetic, on_device(): spread = jnp.mean(shifted * shifted, axis=-1, keepdims=True)  11.6 us
    reduce_sum x1, other arithmetic, on_device(): centre = jnp.mean(source, axis=-1, keepdims=True)  10.7 us
    dot_general x1, matrix products, on_device(): jnp.einsum('hik,hjk->jhi', left, right_all, preferred_element_type=jnp.fl...  10.3 us
    convert_element_type x1, other arithmetic, on_device(): (shifted * lax.rsqrt(spread + 1e-05) * ln_gain + ln_bias).astype(jnp.bflo...  9.28 us
  transfers between devices with their start and end apart: 4, of which 4 were waited for; matrix products, arithmetic and copies ran while one was open for 0% of the time, Pallas kernels for 0%

commit v1 on v0

v1 whole, which is shorter than its diff:
```python
import jax
import jax.numpy as jnp
from jax import lax
from jax.experimental import pallas as pl
from jax.experimental.pallas import tpu as pltpu
from jax.sharding import Mesh, PartitionSpec as P

F32 = jnp.float32
BF16 = jnp.bfloat16
EPS = 1e-05
VMEM_LIMIT = 48 * 1024 * 1024

TILE_I = 256
TILE_K = 64
CH = 128
GROUP = 32
KB = 16


def gate(x):
    return 0.5 * jnp.tanh(0.5 * x) + 0.5


def layer_norm(x, gain, bias):
    centre = jnp.mean(x, axis=-1, keepdims=True)
    shifted = x - centre
    spread = jnp.mean(shifted * shifted, axis=-1, keepdims=True)
    return shifted * lax.rsqrt(spread + EPS) * gain + bias


def project_kernel(
    pair_ref, mask_ref, gain_ref, bias_ref, lv_ref, lg_ref, rv_ref, rg_ref,
    out_ref, weights, valid, normed, staged,
):
    step = pl.program_id(0)

    @pl.when(step == 0)
    def _():
        joined = jnp.concatenate(
            [lv_ref[...], rv_ref[...], lg_ref[...], rg_ref[...]], axis=1
        ).astype(F32)
        weights[...] = joined.T.astype(BF16)
        rows = lax.broadcasted_iota(jnp.int32, (TILE_K, TILE_K), 0)
        cols = lax.broadcasted_iota(jnp.int32, (TILE_K, TILE_K), 1)
        same = jnp.where(rows == cols, 1.0, 0.0).astype(BF16)
        valid[...] = lax.dot_general(
            same, mask_ref[...].astype(F32).astype(BF16),
            (((1,), (1,)), ((), ())), preferred_element_type=F32,
        )

    gain = gain_ref[...].reshape(1, 1, CH)
    bias = bias_ref[...].reshape(1, 1, CH)
    batch = 16

    @pl.loop(0, TILE_I // batch)
    def _(part):
        x = pair_ref[pl.ds(part * batch, batch)].astype(F32)
        n = layer_norm(x, gain, bias)
        normed[pl.ds(part * batch * KB, batch * KB), :] = n.reshape(batch * KB, CH)

    for k in range(KB):
        rows = normed[pl.ds(k, TILE_I, stride=KB), :].astype(BF16)
        y = lax.dot_general(
            weights[...], rows, (((1,), (1,)), ((), ())), preferred_element_type=F32
        )
        kept = valid[pl.ds(step * KB + k, 1), :]
        both = gate(y[2 * GROUP :]) * y[: 2 * GROUP] * kept
        for part in range(2):
            staged[part, pl.ds(k, 2 * GROUP, stride=KB), :] = both[:, part * 128 : (part + 1) * 128]

    for side in range(2):
        for part in range(2):
            block = staged[part, pl.ds(side * GROUP * KB, GROUP * KB), :]
            out_ref[:, side, :, part * 128 : (part + 1) * 128] = block.reshape(GROUP, KB, 128).astype(BF16)


def project(pair, mask, gain, bias, lv, lg, rv, rg):
    whole = lambda *shape: pl.BlockSpec(shape, lambda s: (0,) * len(shape))
    return pl.pallas_call(
        project_kernel,
        grid=(TILE_K // KB,),
        in_specs=[
            pl.BlockSpec((TILE_I, KB, CH), lambda s: (0, s, 0)),
            whole(TILE_I, TILE_K),
            whole(1, CH),
            whole(1, CH),
            whole(CH, GROUP),
            whole(CH, GROUP),
            whole(CH, GROUP),
            whole(CH, GROUP),
        ],
        out_specs=pl.BlockSpec((GROUP, 2, KB, TILE_I), lambda s: (0, 0, s, 0)),
        out_shape=jax.ShapeDtypeStruct((GROUP, 2, TILE_K, TILE_I), BF16),
        scratch_shapes=[
            pltpu.VMEM((CH, CH), BF16),
            pltpu.VMEM((TILE_K, TILE_I), F32),
            pltpu.VMEM((TILE_I * KB, CH), F32),
            pltpu.VMEM((2, 2 * GROUP * KB, 128), F32),
        ],
        compiler_params=pltpu.CompilerParams(vmem_limit_bytes=VMEM_LIMIT),
        cost_estimate=pl.CostEstimate(
            flops=2 * TILE_I * TILE_K * CH * CH, bytes_accessed=7 << 20, transcendentals=1 << 20
        ),
        name="project",
    )(pair, mask, gain, bias, lv, lg, rv, rg)


def gating_kernel(own_ref, pair_ref, gain_ref, bias_ref, weight_ref, out_ref):
    rows = pair_ref.shape[0] * pair_ref.shape[1]
    x = pair_ref[...].astype(F32)
    n = layer_norm(x, gain_ref[...].reshape(1, 1, CH), bias_ref[...].reshape(1, 1, CH))
    n = n.reshape(rows, CH).astype(BF16)
    out_ref[...] = gate(jnp.dot(n, weight_ref[...], preferred_element_type=F32))


def gating(own, pair, gain, bias, weight):
    cols = TILE_K // 4
    batch = 32
    return pl.pallas_call(
        gating_kernel,
        grid_spec=pltpu.PrefetchScalarGridSpec(
            num_scalar_prefetch=1,
            grid=(TILE_I // batch,),
            in_specs=[
                pl.BlockSpec((batch, cols, CH), lambda s, own: (s, own[0], 0)),
                pl.BlockSpec((1, CH), lambda s, own: (0, 0)),
                pl.BlockSpec((1, CH), lambda s, own: (0, 0)),
                pl.BlockSpec((CH, CH), lambda s, own: (0, 0)),
            ],
            out_specs=pl.BlockSpec((batch * cols, CH), lambda s, own: (s, 0)),
        ),
        out_shape=jax.ShapeDtypeStruct((TILE_I * cols, CH), F32),
        compiler_params=pltpu.CompilerParams(vmem_limit_bytes=VMEM_LIMIT),
        cost_estimate=pl.CostEstimate(
            flops=2 * TILE_I * cols * CH * CH, bytes_accessed=3 << 20, transcendentals=1 << 19
        ),
        name="gating",
    )(own, pair, gain, bias, weight)


def product_kernel(core_ref, left_ref, right_ref, other_ref, out_ref):
    core = core_ref[0]
    for which in range(2):
        block = (right_ref, other_ref)[which]
        right = block[...].reshape(1024, TILE_I)
        slot = core if which == 0 else 1 - core
        for z in range(2):
            left = left_ref[z].reshape(1024, TILE_I)
            out_ref[z, 0, slot] = lax.dot_general(
                right, left, (((0,), (0,)), ((), ())), preferred_element_type=F32
            ).astype(BF16)


def product(core, moved, other):
    return pl.pallas_call(
        product_kernel,
        grid_spec=pltpu.PrefetchScalarGridSpec(
            num_scalar_prefetch=1,
            grid=(2,),
            in_specs=[
                pl.BlockSpec((2, 16, 1, TILE_K, TILE_I), lambda s, core: (0, 0, 0, 0, 0)),
                pl.BlockSpec((1, 16, 1, TILE_K, TILE_I), lambda s, core: (s, 0, 1, 0, 0)),
                pl.BlockSpec((1, 16, TILE_K, TILE_I), lambda s, core: (s, 0, 0, 0)),
            ],
            out_specs=pl.BlockSpec((2, 1, 2, TILE_I, TILE_I), lambda s, core: (0, s, 0, 0, 0)),
        ),
        out_shape=jax.ShapeDtypeStruct((2, 2, 2, TILE_I, TILE_I), BF16),
        compiler_params=pltpu.CompilerParams(vmem_limit_bytes=VMEM_LIMIT),
        cost_estimate=pl.CostEstimate(flops=1 << 30, bytes_accessed=4 << 20, transcendentals=0),
        name="product",
    )(core, moved, moved, other)


def finish_kernel(prod_ref, gate_ref, gain_ref, bias_ref, weight_ref, out_ref, hidden, result):
    cols = prod_ref.shape[1]
    lanes = prod_ref.shape[2]
    batch = 8

    def add(part, sums):
        x = prod_ref[pl.ds(part * batch, batch)].astype(F32)
        return sums[0] + jnp.sum(x, axis=0), sums[1] + jnp.sum(x * x, axis=0)

    zero = jnp.zeros((cols, lanes), F32)
    first, second = lax.fori_loop(0, CH // batch, add, (zero, zero))
    mean = first * (1.0 / CH)
    scale = lax.rsqrt(second * (1.0 / CH) - mean * mean + EPS)
    for source in range(CH):
        h = (source % 4) * GROUP + source // 4
        x = prod_ref[source].astype(F32)
        hidden[pl.ds(h * cols, cols), :] = (x - mean) * scale * gain_ref[h] + bias_ref[h]
    for j in range(cols):
        rows = hidden[pl.ds(j, CH, stride=cols), :].astype(BF16)
        mixed = lax.dot_general(
            rows, weight_ref[...], (((0,), (0,)), ((), ())), preferred_element_type=F32
        )
        result[pl.ds(j, lanes, stride=cols), :] = mixed * gate_ref[pl.ds(j, lanes, stride=cols), :]
    out_ref[...] = result[...].reshape(lanes, cols, CH).astype(BF16)


def finish(prod, gates, gain, bias, weight):
    cols = TILE_K // 4
    lanes = 128
    return pl.pallas_call(
        finish_kernel,
        grid=(TILE_I // lanes,),
        in_specs=[
            pl.BlockSpec((CH, cols, lanes), lambda s: (0, 0, s)),
            pl.BlockSpec((lanes * cols, CH), lambda s: (s, 0)),
            pl.BlockSpec(memory_space=pltpu.SMEM),
            pl.BlockSpec(memory_space=pltpu.SMEM),
            pl.BlockSpec((CH, CH), lambda s: (0, 0)),
        ],
        out_specs=pl.BlockSpec((lanes, cols, CH), lambda s: (s, 0, 0)),
        out_shape=jax.ShapeDtypeStruct((TILE_I, cols, CH), BF16),
        scratch_shapes=[
            pltpu.VMEM((CH * cols, lanes), F32),
            pltpu.VMEM((lanes * cols, CH), F32),
        ],
        compiler_params=pltpu.CompilerParams(vmem_limit_bytes=VMEM_LIMIT),
        cost_estimate=pl.CostEstimate(
            flops=2 * TILE_I * cols * CH * CH, bytes_accessed=4 << 20, transcendentals=0
        ),
        name="finish",
    )(prod, gates, gain, bias, weight)


def on_device(
    pair, pair_mask, ln_gain, ln_bias, left_value, left_gate, right_value, right_gate,
    hid_gain, hid_bias, out_weight, out_gate,
):
    gain = ln_gain.reshape(1, CH)
    bias = ln_bias.reshape(1, CH)
    core = lax.axis_index("core").astype(jnp.int32).reshape(1)
    own = lax.axis_index("chan").astype(jnp.int32).reshape(1)
    sides = project(pair, pair_mask, gain, bias, left_value, left_gate, right_value, right_gate)
    moved = lax.all_to_all(sides, ("zl", "x", "y"), 0, 0, tiled=True)
    gates = gating(own, pair, gain, bias, out_gate)
    moved = moved.reshape(2, 16, 2, TILE_K, TILE_I)
    other = lax.ppermute(moved[:, :, 1], "core", [(0, 1), (1, 0)])
    prod = product(core, moved, other).reshape(CH, TILE_K // 4, TILE_I)
    prod = lax.all_to_all(prod, ("zl", "x", "y", "chan"), 0, 0, tiled=True)
    return finish(prod, gates, hid_gain, hid_bias, out_weight)


def solution(mesh):
    split = Mesh(mesh.devices.reshape(2, 2, 4, 4, 4), ("zl", "core", "x", "y", "chan"))
    row, col = ("zl", "core"), ("x", "y")
    return jax.shard_map(
        on_device,
        mesh=split,
        in_specs=(
            P(row, col, None),
            P(row, col),
            P(),
            P(),
            P(None, "chan"),
            P(None, "chan"),
            P(None, "chan"),
            P(None, "chan"),
            P(),
            P(),
            P(),
            P(),
        ),
        out_specs=P(row, ("x", "y", "chan"), None),
        check_vma=False,
    )
```

time: 375 us -> 114 us (0.30)
  waiting for transfers between devices: 301 us -> 24.5 us
  other arithmetic: 40.5 us -> 0 us
  blocking collectives: 0 us -> 35.2 us
  Pallas kernels: 0 us -> 31.5 us
  matrix products: 17 us -> 0 us
  starting transfers between devices: 0.38 us -> 14.3 us
  between operations: 13.3 us -> 0.1 us
  local copies, waits for them, and re-layouts: 2.52 us -> 6.71 us
    reduce_scatter x2 -> x0, waiting for transfers between devices: 200 us -> none  [the longest x1 115 us: on_device(): lax.psum_scatter(jnp.einsum('hik,hjk->jhi', left, right_all, preferred_el...]
    all_gather x1 -> x0, waiting for transfers between devices: 53.4 us -> none  [on_device(): right_all = lax.all_gather(right, 'row', axis=1, tiled=True)]
    psum x1 -> x0, waiting for transfers between devices: 47.2 us -> none  [on_device(): lax.psum(second_sums.astype(jnp.bfloat16), 'chan').astype(jnp.float32)]
    all_to_all x0 -> x1, blocking collectives: none -> 35.2 us  [on_device(): moved = lax.all_to_all(sides, ('zl', 'x', 'y'), 0, 0, tiled=True)]
    pallas_call x0 -> x4, Pallas kernels: none -> 31.5 us  [the longest x1 19.2 us: project(): pl.pallas_call(project_kernel, grid=(TILE_K // KB,), in_specs=[pl.BlockSp...]
    reduce_sum x4 -> x0, other arithmetic: 26.4 us -> none  [the longest x1 11.6 us: on_device(): spread = jnp.mean(shifted * shifted, axis=-1, keepdims=True)]
    all_to_all x0 -> x1, waiting for transfers between devices: none -> 22 us  [on_device(): prod = lax.all_to_all(prod, ('zl', 'x', 'y', 'chan'), 0, 0, tiled=True)]
    dot_general x4 -> x0, matrix products: 17 us -> none  [the longest x1 10.3 us: on_device(): jnp.einsum('hik,hjk->jhi', left, right_all, preferred_element_type=jnp.fl...]
  transfers between devices with their start and end apart: 4 -> 2, of which waited for: 4 -> 2; matrix products, arithmetic and copies ran while one was open for 0% -> 0% of each run, Pallas kernels for 0% -> 5%
where the time goes in v1:
time: 114 us; the launch traced here: 112 us
  blocking collectives  35.2 us (31%)
  Pallas kernels  31.5 us (28%)
  waiting for transfers between devices  24.5 us (21%)
  starting transfers between devices  14.3 us (13%)
  local copies, waits for them, and re-layouts  6.71 us (6%)
    all_to_all x1, blocking collectives, on_device(): moved = lax.all_to_all(sides, ('zl', 'x', 'y'), 0, 0, tiled=True)  35.2 us
    all_to_all x1, waiting for transfers between devices, on_device(): prod = lax.all_to_all(prod, ('zl', 'x', 'y', 'chan'), 0, 0, tiled=True)  22 us
    pallas_call x1, Pallas kernels, project(): pl.pallas_call(project_kernel, grid=(TILE_K // KB,), in_specs=[pl.BlockSp...  19.2 us
    all_to_all x1, starting transfers between devices, on_device(): prod = lax.all_to_all(prod, ('zl', 'x', 'y', 'chan'), 0, 0, tiled=True)  11.8 us
    pallas_call x1, Pallas kernels, gating(): pl.pallas_call(gating_kernel, grid_spec=pltpu.PrefetchScalarGridSpec(num_...  5.58 us
    unnamed x21, local copies, waits for them, and re-layouts  5.53 us
    pallas_call x1, Pallas kernels, finish(): pl.pallas_call(finish_kernel, grid=(TILE_I // lanes,), in_specs=[pl.Block...  4.29 us
    ppermute x1, starting transfers between devices, on_device(): other = lax.ppermute(moved[:, :, 1], 'core', [(0, 1), (1, 0)])  2.53 us
  transfers between devices with their start and end apart: 2, of which 2 were waited for; matrix products, arithmetic and copies ran while one was open for 0% of the time, Pallas kernels for 5%

profile of v1, /device:TPU:1, one launch (start us, length us, event | category | flops | bytes accessed | tf_op | source)
XLA Modules:
  0.0 112.3 jit_solution(9049583888465533055)
XLA Ops:
  0.0 0.9 copy.13.mask_ref
  0.9 0.8 copy.14.lv_ref
  1.7 0.8 copy.15.lg_ref
  2.6 0.8 copy.16.rv_ref
  3.4 0.8 copy.17.rg_ref
  4.2 0.0 copy-start.2
  4.2 0.7 copy-done.2
  4.9 0.0 copy-start.4
  4.9 0.7 copy-done.4
  5.5 19.2 %project.1 = bf16[32,2,64,256]{3,2,1,0:T(8,128)(2,1)S(1)} custom-call(bf16[256,64,128]{2,1,0:T(8,128)(2,1)} %pair_ref.3, s32[256,64]{1,0:T(8,128)S(1)} %copy.13.mask_ref, f32[1,128]{1,0:T(1,128)S(1)} %bitcast.11, f32[1,128]{1,0:T(1,128)S(1)} %bitcast.13, bf16[128,32]{1,0:T(8,128)(2,1)S(1)} %copy.14.lv_ref, bf16[128,32]{1,0:T(8,128)(2,1)S(1)} %copy.15.lg_ref, ...), custom_call_target="tpu_custom_call" | custom-call | flops 536870912 | bytes 7340032 | tf_op jit(solution)/shard_map/project/pallas_call | solution.py:79
  24.7 35.2 %all_to_all.10 = bf16[32,2,64,256]{3,2,1,0:T(8,128)(2,1)S(1)} all-to-all(bf16[32,2,64,256]{3,2,1,0:T(8,128)(2,1)S(1)} %project.1), channel_id=1, replica_groups=mesh['zl'=2,'core'=2,'x'=4,'y'=4,'chan'=4] {'zl','x','y'}, dimensions={0} | all-to-all | bytes 4194304 | tf_op jit(solution)/shard_map/all_to_all | solution.py:236
  59.9 0.1 copy.18
  60.1 1.0 slice_bitcast_fusion
  61.1 2.5 %collective-permute-start = (bf16[2,16,64,256]{3,2,1,0:T(8,128)(2,1)}, bf16[2,16,64,256]{3,2,1,0:T(8,128)(2,1)S(1)}, u32[]{:S(2)}, u32[]{:S(2)}) collective-permute-start(bf16[2,16,64,256]{3,2,1,0:T(8,128)(2,1)} %slice_bitcast_fusion), channel_id=1, source_target_pairs={{0,64},{64,0},{1,65},{65,1},{2,66},{66,2},{3,67},{67,3},{4,68},{68... | collective-permute-start | bytes 3145736 | tf_op jit(solution)/shard_map/ppermute | solution.py:239
  63.6 2.5 %collective-permute-done.other_ref = bf16[2,16,64,256]{3,2,1,0:T(8,128)(2,1)S(1)} collective-permute-done((bf16[2,16,64,256]{3,2,1,0:T(8,128)(2,1)}, bf16[2,16,64,256]{3,2,1,0:T(8,128)(2,1)S(1)}, u32[]{:S(2)}, u32[]{:S(2)}) %collective-permute-start) | collective-permute-done | bytes 1048608 | tf_op jit(solution)/shard_map/ppermute | solution.py:239
  66.1 2.5 %product.1 = bf16[2,2,2,256,256]{4,3,2,1,0:T(8,128)(2,1)} custom-call(s32[1]{0:T(128)} %bitcast.core_ref, bf16[2,16,2,64,256]{4,3,2,1,0:T(8,128)(2,1)S(1)} %bitcast.9, bf16[2,16,2,64,256]{4,3,2,1,0:T(8,128)(2,1)S(1)} %bitcast.10, bf16[2,16,64,256]{3,2,1,0:T(8,128)(2,1)S(1)} %collective-permute-done.other_ref), custom_call_target="tpu_custom_call" | custom-call | flops 1073741824 | bytes 4194304 | tf_op jit(solution)/shard_map/product/pallas_call | solution.py:155
  68.6 0.0 copy-start
  68.6 0.0 copy-start.3
  68.6 0.0 copy-start.5
  68.6 11.8 %all-to-all-start.1 = ((bf16[128,16,256]{2,1,0:T(8,128)(2,1)}), bf16[128,16,256]{2,1,0:T(8,128)(2,1)S(1)}, u32[]{:S(2)}, u32[]{:S(2)}) async-start(bf16[128,16,256]{2,1,0:T(8,128)(2,1)} %bitcast.6), calls=%async_computation.1 | async-start | bytes 2097152 | tf_op jit(solution)/shard_map/all_to_all | solution.py:241
  80.4 0.0 copy-done
  80.4 0.0 copy-done.3
  80.4 0.0 copy-done.5
  80.4 0.0 copy-start.1
  80.4 0.0 copy-start.6
  80.4 0.0 copy-start.7
  80.5 5.6 %gating.1.gate_ref = f32[4096,128]{1,0:T(8,128)S(1)} custom-call(s32[1]{0:T(128)} %bitcast.7.own_ref, bf16[256,64,128]{2,1,0:T(8,128)(2,1)} %pair_ref.3, f32[1,128]{1,0:T(1,128)S(1)} %bitcast.12, f32[1,128]{1,0:T(1,128)S(1)} %bitcast.14, bf16[128,128]{1,0:T(8,128)(2,1)S(1)} %copy-done), custom_call_target="tpu_custom_call" | custom-call | flops 134217728 | bytes 3145728 | tf_op jit(solution)/shard_map/gating/pallas_call | solution.py:119
  86.0 22.0 %all-to-all-done.1.prod_ref = bf16[128,16,256]{2,1,0:T(8,128)(2,1)S(1)} async-done(((bf16[128,16,256]{2,1,0:T(8,128)(2,1)}), bf16[128,16,256]{2,1,0:T(8,128)(2,1)S(1)}, u32[]{:S(2)}, u32[]{:S(2)}) %all-to-all-start.1) | async-done | bytes 1048608 | tf_op jit(solution)/shard_map/all_to_all | solution.py:241
  108.0 0.0 copy-done.1
  108.0 0.0 copy-done.6
  108.0 0.0 copy-done.7
  108.0 4.3 %finish.1 = bf16[256,16,128]{2,1,0:T(8,128)(2,1)} custom-call(bf16[128,16,256]{2,1,0:T(8,128)(2,1)S(1)} %all-to-all-done.1.prod_ref, f32[4096,128]{1,0:T(8,128)S(1)} %gating.1.gate_ref, f32[128]{0:T(128)S(1)} %copy-done.6, f32[128]{0:T(128)S(1)} %copy-done.7, bf16[128,128]{1,0:T(8,128)(2,1)S(1)} %copy-done.1), custom_call_target="tpu_custom_call" | custom-call | flops 134217728 | bytes 4194304 | tf_op jit(solution)/shard_map/finish/pallas_call | solution.py:203
Async XLA Ops:
  4.2 0.7 copy-start.2
  4.9 0.7 copy-start.4
  61.1 5.0 %collective-permute-start = (bf16[2,16,64,256]{3,2,1,0:T(8,128)(2,1)}, bf16[2,16,64,256]{3,2,1,0:T(8,128)(2,1)S(1)}, u32[]{:S(2)}, u32[]{:S(2)}) collective-permute-start(bf16[2,16,64,256]{3,2,1,0:T(8,128)(2,1)} %slice_bitcast_fusion), channel_id=1, source_target_pairs={{0,64},{64,0},{1,65},{65,1},{2,66},{66,2},{3,67},{67,3},{4,68},{68... | collective-permute-start | bytes 3145736 | tf_op jit(solution)/shard_map/ppermute | solution.py:239
  68.6 11.8 %copy-start = (bf16[128,128]{1,0:T(8,128)(2,1)S(1)}, bf16[128,128]{1,0:T(8,128)(2,1)}, u32[]{:S(2)}) copy-start(bf16[128,128]{1,0:T(8,128)(2,1)} %weight_ref.2) | copy-start | bytes 98308
  68.6 11.8 %copy-start.3 = (f32[128]{0:T(128)S(1)}, f32[128]{0:T(128)}, u32[]{:S(2)}) copy-start(f32[128]{0:T(128)} %param.14) | copy-start | bytes 1540
  68.6 11.8 %copy-start.5 = (f32[128]{0:T(128)S(1)}, f32[128]{0:T(128)}, u32[]{:S(2)}) copy-start(f32[128]{0:T(128)} %param.15) | copy-start | bytes 1540
  68.6 39.4 %all-to-all-start.1 = ((bf16[128,16,256]{2,1,0:T(8,128)(2,1)}), bf16[128,16,256]{2,1,0:T(8,128)(2,1)S(1)}, u32[]{:S(2)}, u32[]{:S(2)}) async-start(bf16[128,16,256]{2,1,0:T(8,128)(2,1)} %bitcast.6), calls=%async_computation.1 | async-start | bytes 2097152 | tf_op jit(solution)/shard_map/all_to_all | solution.py:241
  80.4 27.6 %copy-start.1 = (bf16[128,128]{1,0:T(8,128)(2,1)S(1)}, bf16[128,128]{1,0:T(8,128)(2,1)}, u32[]{:S(2)}) copy-start(bf16[128,128]{1,0:T(8,128)(2,1)} %weight_ref.3) | copy-start | bytes 98308
  80.4 27.6 %copy-start.6 = (f32[128]{0:T(128)S(1)}, f32[128]{0:T(128)}, u32[]{:S(2)}) copy-start(f32[128]{0:T(128)} %gain_ref.1) | copy-start | bytes 1540
  80.4 27.6 %copy-start.7 = (f32[128]{0:T(128)S(1)}, f32[128]{0:T(128)}, u32[]{:S(2)}) copy-start(f32[128]{0:T(128)} %bias_ref.1) | copy-start | bytes 1540

commit v2 on v1

v2 whole, which is shorter than its diff:
```python
import jax
import jax.numpy as jnp
from jax import lax
from jax.experimental import pallas as pl
from jax.experimental.pallas import tpu as pltpu
from jax.sharding import Mesh, PartitionSpec as P

F32 = jnp.float32
BF16 = jnp.bfloat16
EPS = 1e-05
VMEM_LIMIT = 48 * 1024 * 1024
PROJECT_LIMIT = 60 * 1024 * 1024

TILE_I = 256
TILE_K = 64
CH = 128
GROUP = 32
KB = 16
PITCH = 24


def layer_norm(x, gain, bias):
    centre = jnp.mean(x, axis=-1, keepdims=True)
    shifted = x - centre
    spread = jnp.mean(shifted * shifted, axis=-1, keepdims=True)
    return shifted * lax.rsqrt(spread + EPS) * gain + bias


def whole(*shape):
    return pl.BlockSpec(shape, lambda *s: (0,) * len(shape))


def project_kernel(
    pair_ref, mask_ref, gain_ref, bias_ref, lv_ref, lg_ref, rv_ref, rg_ref, out_ref, normed, staged
):
    step = pl.program_id(0)
    gain, bias = gain_ref[...], bias_ref[...]
    half = jnp.asarray(0.5, BF16)
    weights = jnp.concatenate([lv_ref[...], rv_ref[...], lg_ref[...], rg_ref[...]], axis=0) * half
    flat = normed.reshape(TILE_I * PITCH, CH)
    flat_staged = staged.reshape(2 * 2 * GROUP * PITCH, 128)
    batch = 64
    for part in range(TILE_I // batch):
        x = pair_ref[part * batch : (part + 1) * batch].astype(F32).reshape(batch * KB, CH)
        n = layer_norm(x, gain, bias)
        normed[part * batch : (part + 1) * batch, :KB, :] = n.reshape(batch, KB, CH)
    for k in range(KB):
        rows = flat[pl.ds(k, TILE_I, stride=PITCH), :].astype(BF16)
        y = lax.dot_general(
            weights, rows, (((1,), (1,)), ((), ())), preferred_element_type=F32
        )
        kept = mask_ref[pl.ds(step * KB + k, 1), :].astype(F32)
        sides = (jnp.tanh(y[2 * GROUP :]) + 1.0) * (y[: 2 * GROUP] * kept)
        for part in range(2):
            first = part * 2 * GROUP * PITCH + k
            flat_staged[pl.ds(first, 2 * GROUP, stride=PITCH), :] = sides[:, part * 128 : (part + 1) * 128]
    for side in range(2):
        for part in range(2):
            block = staged[part, side * GROUP : (side + 1) * GROUP, :KB, :]
            out_ref[:, side, :, part * 128 : (part + 1) * 128] = block.astype(BF16)


def project(pair, mask, gain, bias, lv, lg, rv, rg):
    return pl.pallas_call(
        project_kernel,
        grid=(TILE_K // KB,),
        in_specs=[
            pl.BlockSpec((TILE_I, KB, CH), lambda s: (0, s, 0)),
            whole(TILE_K, TILE_I),
            whole(1, CH),
            whole(1, CH),
            whole(GROUP, CH),
            whole(GROUP, CH),
            whole(GROUP, CH),
            whole(GROUP, CH),
        ],
        out_specs=pl.BlockSpec((GROUP, 2, KB, TILE_I), lambda s: (0, 0, s, 0)),
        out_shape=jax.ShapeDtypeStruct((GROUP, 2, TILE_K, TILE_I), BF16),
        scratch_shapes=[
            pltpu.VMEM((TILE_I, PITCH, CH), F32),
            pltpu.VMEM((2, 2 * GROUP, PITCH, 128), F32),
        ],
        compiler_params=pltpu.CompilerParams(vmem_limit_bytes=PROJECT_LIMIT),
        cost_estimate=pl.CostEstimate(
            flops=2 * TILE_I * TILE_K * CH * CH, bytes_accessed=7 << 20, transcendentals=1 << 20
        ),
        name="project",
    )(pair, mask, gain, bias, lv, lg, rv, rg)


def gating_kernel(own_ref, pair_ref, gain_ref, bias_ref, weight_ref, out_ref, normed):
    batch, cols, _ = pair_ref.shape
    x = pair_ref[...].astype(F32).reshape(batch * cols, CH)
    n = layer_norm(x, gain_ref[...], bias_ref[...])
    normed[:, :cols, :] = n.reshape(batch, cols, CH)
    flat = normed.reshape(batch * PITCH, CH)
    for j in range(cols):
        rows = flat[pl.ds(j, batch, stride=PITCH), :].astype(BF16)
        y = jnp.dot(rows, weight_ref[...], preferred_element_type=F32)
        out_ref[j] = 0.5 * jnp.tanh(0.5 * y) + 0.5


def gating(own, pair, gain, bias, weight):
    cols = TILE_K // 4
    batch = 64
    return pl.pallas_call(
        gating_kernel,
        grid_spec=pltpu.PrefetchScalarGridSpec(
            num_scalar_prefetch=1,
            grid=(TILE_I // batch,),
            in_specs=[
                pl.BlockSpec((batch, cols, CH), lambda s, own: (s, own[0], 0)),
                whole(1, CH),
                whole(1, CH),
                whole(CH, CH),
            ],
            out_specs=pl.BlockSpec((cols, batch, CH), lambda s, own: (0, s, 0)),
            scratch_shapes=[pltpu.VMEM((batch, PITCH, CH), F32)],
        ),
        out_shape=jax.ShapeDtypeStruct((cols, TILE_I, CH), F32),
        compiler_params=pltpu.CompilerParams(vmem_limit_bytes=VMEM_LIMIT),
        cost_estimate=pl.CostEstimate(
            flops=2 * TILE_I * cols * CH * CH, bytes_accessed=3 << 20, transcendentals=1 << 19
        ),
        name="gating",
    )(own, pair, gain, bias, weight)


def product_kernel(core_ref, left_ref, right_ref, other_ref, out_ref):
    core = core_ref[0]
    for which in range(2):
        block = (right_ref, other_ref)[which]
        right = block[...].reshape(1024, TILE_I)
        slot = core if which == 0 else 1 - core
        for z in range(2):
            left = left_ref[z].reshape(1024, TILE_I)
            out_ref[z, 0, slot] = lax.dot_general(
                right, left, (((0,), (0,)), ((), ())), preferred_element_type=F32
            ).astype(BF16)


def product(core, moved, other):
    return pl.pallas_call(
        product_kernel,
        grid_spec=pltpu.PrefetchScalarGridSpec(
            num_scalar_prefetch=1,
            grid=(2,),
            in_specs=[
                pl.BlockSpec((2, 16, 1, TILE_K, TILE_I), lambda s, core: (0, 0, 0, 0, 0)),
                pl.BlockSpec((1, 16, 1, TILE_K, TILE_I), lambda s, core: (s, 0, 1, 0, 0)),
                pl.BlockSpec((1, 16, TILE_K, TILE_I), lambda s, core: (s, 0, 0, 0)),
            ],
            out_specs=pl.BlockSpec((2, 1, 2, TILE_I, TILE_I), lambda s, core: (0, s, 0, 0, 0)),
        ),
        out_shape=jax.ShapeDtypeStruct((2, 2, 2, TILE_I, TILE_I), BF16),
        compiler_params=pltpu.CompilerParams(vmem_limit_bytes=VMEM_LIMIT),
        cost_estimate=pl.CostEstimate(flops=1 << 30, bytes_accessed=4 << 20, transcendentals=0),
        name="product",
    )(core, moved, moved, other)


def finish_kernel(prod_ref, gate_ref, gain_ref, bias_ref, weight_ref, out_ref, hidden, result):
    cols = prod_ref.shape[1]
    lanes = prod_ref.shape[2]
    batch = 8

    def add(part, sums):
        x = prod_ref[pl.ds(part * batch, batch)].astype(F32)
        return sums[0] + jnp.sum(x, axis=0), sums[1] + jnp.sum(x * x, axis=0)

    zero = jnp.zeros((cols, lanes), F32)
    first, second = lax.fori_loop(0, CH // batch, add, (zero, zero))
    mean = first * (1.0 / CH)
    scale = lax.rsqrt(second * (1.0 / CH) - mean * mean + EPS)
    flat_hidden = hidden.reshape(CH * PITCH, lanes)
    flat_result = result.reshape(lanes * PITCH, CH)
    for source in range(CH):
        h = (source % 4) * GROUP + source // 4
        x = prod_ref[source].astype(F32)
        hidden[h, :cols, :] = (x - mean) * scale * gain_ref[h] + bias_ref[h]
    for j in range(cols):
        rows = flat_hidden[pl.ds(j, CH, stride=PITCH), :].astype(BF16)
        mixed = lax.dot_general(
            rows, weight_ref[...], (((0,), (0,)), ((), ())), preferred_element_type=F32
        )
        flat_result[pl.ds(j, lanes, stride=PITCH), :] = mixed * gate_ref[j]
    out_ref[...] = result[:, :cols, :].astype(BF16)


def finish(prod, gates, gain, bias, weight):
    cols = TILE_K // 4
    lanes = 128
    return pl.pallas_call(
        finish_kernel,
        grid=(TILE_I // lanes,),
        in_specs=[
            pl.BlockSpec((CH, cols, lanes), lambda s: (0, 0, s)),
            pl.BlockSpec((cols, lanes, CH), lambda s: (0, s, 0)),
            pl.BlockSpec(memory_space=pltpu.SMEM),
            pl.BlockSpec(memory_space=pltpu.SMEM),
            pl.BlockSpec((CH, CH), lambda s: (0, 0)),
        ],
        out_specs=pl.BlockSpec((lanes, cols, CH), lambda s: (s, 0, 0)),
        out_shape=jax.ShapeDtypeStruct((TILE_I, cols, CH), BF16),
        scratch_shapes=[
            pltpu.VMEM((CH, PITCH, lanes), F32),
            pltpu.VMEM((lanes, PITCH, CH), F32),
        ],
        compiler_params=pltpu.CompilerParams(vmem_limit_bytes=VMEM_LIMIT),
        cost_estimate=pl.CostEstimate(
            flops=2 * TILE_I * cols * CH * CH, bytes_accessed=4 << 20, transcendentals=0
        ),
        name="finish",
    )(prod, gates, gain, bias, weight)


def on_device(
    pair, pair_mask, ln_gain, ln_bias, left_value, left_gate, right_value, right_gate,
    hid_gain, hid_bias, out_weight, out_gate,
):
    gain = ln_gain.reshape(1, CH)
    bias = ln_bias.reshape(1, CH)
    core = lax.axis_index("core").astype(jnp.int32).reshape(1)
    own = lax.axis_index("chan").astype(jnp.int32).reshape(1)
    sides = project(
        pair, pair_mask.T, gain, bias, left_value.T, left_gate.T, right_value.T, right_gate.T
    )
    moved = lax.all_to_all(sides, ("zl", "x", "y"), 0, 0, tiled=True)
    moved = moved.reshape(2, 16, 2, TILE_K, TILE_I)
    other = lax.ppermute(moved[:, :, 1], "core", [(0, 1), (1, 0)])
    gates = gating(own, pair, gain, bias, out_gate)
    prod = product(core, moved, other).reshape(CH, TILE_K // 4, TILE_I)
    prod = lax.all_to_all(prod, ("zl", "x", "y", "chan"), 0, 0, tiled=True)
    return finish(prod, gates, hid_gain, hid_bias, out_weight)


def solution(mesh):
    split = Mesh(mesh.devices.reshape(2, 2, 4, 4, 4), ("zl", "core", "x", "y", "chan"))
    row, col = ("zl", "core"), ("x", "y")
    return jax.shard_map(
        on_device,
        mesh=split,
        in_specs=(
            P(row, col, None),
            P(row, col),
            P(),
            P(),
            P(None, "chan"),
            P(None, "chan"),
            P(None, "chan"),
            P(None, "chan"),
            P(),
            P(),
            P(),
            P(),
        ),
        out_specs=P(row, ("x", "y", "chan"), None),
        check_vma=False,
    )
```

time: 114 us -> 98.1 us (0.86)
  Pallas kernels: 31.5 us -> 19.3 us
  local copies, waits for them, and re-layouts: 6.71 us -> 1.2 us
  waiting for transfers between devices: 24.5 us -> 26.1 us
    pallas_call x1, Pallas kernels: 19.2 us -> 9.57 us  [project(): pl.pallas_call(project_kernel, grid=(TILE_K // KB,), in_specs=[pl.BlockSp...]
    unnamed x21 -> x12, local copies, waits for them, and re-layouts: 5.53 us -> 0.03 us
    all_to_all x1, waiting for transfers between devices: 22 us -> 23.6 us  [on_device(): prod = lax.all_to_all(prod, ('zl', 'x', 'y', 'chan'), 0, 0, tiled=True)]
    pallas_call x1, Pallas kernels: 5.58 us -> 3.92 us  [gating(): pl.pallas_call(gating_kernel, grid_spec=pltpu.PrefetchScalarGridSpec(num_...]
  transfers between devices with their start and end apart: 2 -> 2, of which waited for: 2 -> 2; matrix products, arithmetic and copies ran while one was open for 0% -> 0% of each run, Pallas kernels for 5% -> 4%
where the time goes in v2:
time: 98.1 us; the launch traced here: 96.4 us
  blocking collectives  35.4 us (36%)
  waiting for transfers between devices  26.1 us (27%)
  Pallas kernels  19.3 us (20%)
  starting transfers between devices  14.3 us (15%)
  local copies, waits for them, and re-layouts  1.2 us (1%)
    all_to_all x1, blocking collectives, on_device(): moved = lax.all_to_all(sides, ('zl', 'x', 'y'), 0, 0, tiled=True)  35.4 us
    all_to_all x1, waiting for transfers between devices, on_device(): prod = lax.all_to_all(prod, ('zl', 'x', 'y', 'chan'), 0, 0, tiled=True)  23.6 us
    all_to_all x1, starting transfers between devices, on_device(): prod = lax.all_to_all(prod, ('zl', 'x', 'y', 'chan'), 0, 0, tiled=True)  11.8 us
    pallas_call x1, Pallas kernels, project(): pl.pallas_call(project_kernel, grid=(TILE_K // KB,), in_specs=[pl.BlockSp...  9.57 us
    pallas_call x1, Pallas kernels, gating(): pl.pallas_call(gating_kernel, grid_spec=pltpu.PrefetchScalarGridSpec(num_...  3.92 us
    pallas_call x1, Pallas kernels, finish(): pl.pallas_call(finish_kernel, grid=(TILE_I // lanes,), in_specs=[pl.Block...  3.32 us
    ppermute x1, starting transfers between devices, on_device(): other = lax.ppermute(moved[:, :, 1], 'core', [(0, 1), (1, 0)])  2.53 us
    ppermute x1, waiting for transfers between devices, on_device(): other = lax.ppermute(moved[:, :, 1], 'core', [(0, 1), (1, 0)])  2.5 us
  transfers between devices with their start and end apart: 2, of which 2 were waited for; matrix products, arithmetic and copies ran while one was open for 0% of the time, Pallas kernels for 4%

profile of v2, /device:TPU:1, one launch (start us, length us, event | category | flops | bytes accessed | tf_op | source)
XLA Modules:
  0.0 96.4 jit_solution(9103710900982254377)
XLA Ops:
  0.0 9.6 %project.1 = bf16[32,2,64,256]{3,2,1,0:T(8,128)(2,1)} custom-call(bf16[256,64,128]{2,1,0:T(8,128)(2,1)} %pair_ref.3, s32[64,256]{1,0:T(8,128)} %bitcast.21, f32[1,128]{1,0:T(1,128)} %bitcast.16, f32[1,128]{1,0:T(1,128)} %bitcast.18, bf16[32,128]{1,0:T(8,128)(2,1)} %bitcast.22, bf16[32,128]{1,0:T(8,128)(2,1)} %bitcast.23, bf16[32,128]{1,0:T(8,128)(2,1)} %bitcast.24, ...), custom_call_target="tpu_custom_call" | custom-call | flops 536870912 | bytes 7340032 | tf_op jit(solution)/shard_map/project/pallas_call | solution.py:64
  9.6 35.4 %all_to_all.10 = bf16[32,2,64,256]{3,2,1,0:T(8,128)(2,1)S(1)} all-to-all(bf16[32,2,64,256]{3,2,1,0:T(8,128)(2,1)} %project.1), channel_id=1, replica_groups=mesh['zl'=2,'core'=2,'x'=4,'y'=4,'chan'=4] {'zl','x','y'}, dimensions={0} | all-to-all | bytes 4194304 | tf_op jit(solution)/shard_map/all_to_all | solution.py:228
  45.0 0.1 copy.13
  45.1 1.0 %slice_bitcast_fusion = bf16[2,16,64,256]{3,2,1,0:T(8,128)(2,1)} fusion(bf16[2,16,2,64,256]{4,3,1,0,2:T(8,128)(2,1)S(1)} %bitcast.20), kind=kLoop, calls=%fused_computation | loop fusion | bytes 2097152 | tf_op jit(solution)/shard_map/squeeze | solution.py:230
  46.1 2.5 %collective-permute-start = (bf16[2,16,64,256]{3,2,1,0:T(8,128)(2,1)}, bf16[2,16,64,256]{3,2,1,0:T(8,128)(2,1)S(1)}, u32[]{:S(2)}, u32[]{:S(2)}) collective-permute-start(bf16[2,16,64,256]{3,2,1,0:T(8,128)(2,1)} %slice_bitcast_fusion), channel_id=1, source_target_pairs={{0,64},{64,0},{1,65},{65,1},{2,66},{66,2},{3,67},{67,3},{4,68},{68... | collective-permute-start | bytes 3145736 | tf_op jit(solution)/shard_map/ppermute | solution.py:230
  48.7 2.5 %collective-permute-done.other_ref = bf16[2,16,64,256]{3,2,1,0:T(8,128)(2,1)S(1)} collective-permute-done((bf16[2,16,64,256]{3,2,1,0:T(8,128)(2,1)}, bf16[2,16,64,256]{3,2,1,0:T(8,128)(2,1)S(1)}, u32[]{:S(2)}, u32[]{:S(2)}) %collective-permute-start) | collective-permute-done | bytes 1048608 | tf_op jit(solution)/shard_map/ppermute | solution.py:230
  51.2 2.5 %product.1 = bf16[2,2,2,256,256]{4,3,2,1,0:T(8,128)(2,1)} custom-call(s32[1]{0:T(128)} %bitcast.core_ref, bf16[2,16,2,64,256]{4,3,2,1,0:T(8,128)(2,1)S(1)} %bitcast.14, bf16[2,16,2,64,256]{4,3,2,1,0:T(8,128)(2,1)S(1)} %bitcast.15, bf16[2,16,64,256]{3,2,1,0:T(8,128)(2,1)S(1)} %collective-permute-done.other_ref), custom_call_target="tpu_custom_call" | custom-call | flops 1073741824 | bytes 4194304 | tf_op jit(solution)/shard_map/product/pallas_call | solution.py:143
  53.6 0.0 copy-start
  53.6 0.0 copy-start.2
  53.6 0.0 copy-start.3
  53.6 11.8 %all-to-all-start.1 = ((bf16[128,16,256]{2,1,0:T(8,128)(2,1)}), bf16[128,16,256]{2,1,0:T(8,128)(2,1)S(1)}, u32[]{:S(2)}, u32[]{:S(2)}) async-start(bf16[128,16,256]{2,1,0:T(8,128)(2,1)} %bitcast.11), calls=%async_computation.1 | async-start | bytes 2097152 | tf_op jit(solution)/shard_map/all_to_all | solution.py:233
  65.4 0.0 copy-done
  65.4 0.0 copy-done.2
  65.4 0.0 copy-done.3
  65.4 0.0 copy-start.1
  65.4 0.0 copy-start.4
  65.5 0.0 copy-start.5
  65.5 3.9 %gating.1.gate_ref = f32[16,256,128]{2,1,0:T(8,128)S(1)} custom-call(s32[1]{0:T(128)} %bitcast.12.own_ref, bf16[256,64,128]{2,1,0:T(8,128)(2,1)} %pair_ref.3, f32[1,128]{1,0:T(1,128)S(1)} %bitcast.17, f32[1,128]{1,0:T(1,128)S(1)} %bitcast.19, bf16[128,128]{1,0:T(8,128)(2,1)S(1)} %copy-done), custom_call_target="tpu_custom_call" | custom-call | flops 134217728 | bytes 3145728 | tf_op jit(solution)/shard_map/gating/pallas_call | solution.py:106
  69.4 23.6 %all-to-all-done.1.prod_ref = bf16[128,16,256]{2,1,0:T(8,128)(2,1)S(1)} async-done(((bf16[128,16,256]{2,1,0:T(8,128)(2,1)}), bf16[128,16,256]{2,1,0:T(8,128)(2,1)S(1)}, u32[]{:S(2)}, u32[]{:S(2)}) %all-to-all-start.1) | async-done | bytes 1048608 | tf_op jit(solution)/shard_map/all_to_all | solution.py:233
  93.0 0.0 copy-done.1
  93.0 0.0 copy-done.4
  93.0 0.0 copy-done.5
  93.0 3.3 %finish.1 = bf16[256,16,128]{2,1,0:T(8,128)(2,1)} custom-call(bf16[128,16,256]{2,1,0:T(8,128)(2,1)S(1)} %all-to-all-done.1.prod_ref, f32[16,256,128]{2,1,0:T(8,128)S(1)} %gating.1.gate_ref, f32[128]{0:T(128)S(1)} %copy-done.4, f32[128]{0:T(128)S(1)} %copy-done.5, bf16[128,128]{1,0:T(8,128)(2,1)S(1)} %copy-done.1), custom_call_target="tpu_custom_call" | custom-call | flops 134217728 | bytes 4194304 | tf_op jit(solution)/shard_map/finish/pallas_call | solution.py:193
Async XLA Ops:
  46.1 5.0 %collective-permute-start = (bf16[2,16,64,256]{3,2,1,0:T(8,128)(2,1)}, bf16[2,16,64,256]{3,2,1,0:T(8,128)(2,1)S(1)}, u32[]{:S(2)}, u32[]{:S(2)}) collective-permute-start(bf16[2,16,64,256]{3,2,1,0:T(8,128)(2,1)} %slice_bitcast_fusion), channel_id=1, source_target_pairs={{0,64},{64,0},{1,65},{65,1},{2,66},{66,2},{3,67},{67,3},{4,68},{68... | collective-permute-start | bytes 3145736 | tf_op jit(solution)/shard_map/ppermute | solution.py:230
  53.6 11.8 %copy-start = (bf16[128,128]{1,0:T(8,128)(2,1)S(1)}, bf16[128,128]{1,0:T(8,128)(2,1)}, u32[]{:S(2)}) copy-start(bf16[128,128]{1,0:T(8,128)(2,1)} %weight_ref.2) | copy-start | bytes 98308
  53.6 11.8 %copy-start.2 = (f32[128]{0:T(128)S(1)}, f32[128]{0:T(128)}, u32[]{:S(2)}) copy-start(f32[128]{0:T(128)} %param.14) | copy-start | bytes 1540
  53.6 11.8 %copy-start.3 = (f32[128]{0:T(128)S(1)}, f32[128]{0:T(128)}, u32[]{:S(2)}) copy-start(f32[128]{0:T(128)} %param.15) | copy-start | bytes 1540
  53.6 39.4 %all-to-all-start.1 = ((bf16[128,16,256]{2,1,0:T(8,128)(2,1)}), bf16[128,16,256]{2,1,0:T(8,128)(2,1)S(1)}, u32[]{:S(2)}, u32[]{:S(2)}) async-start(bf16[128,16,256]{2,1,0:T(8,128)(2,1)} %bitcast.11), calls=%async_computation.1 | async-start | bytes 2097152 | tf_op jit(solution)/shard_map/all_to_all | solution.py:233
  65.4 27.6 %copy-start.1 = (bf16[128,128]{1,0:T(8,128)(2,1)S(1)}, bf16[128,128]{1,0:T(8,128)(2,1)}, u32[]{:S(2)}) copy-start(bf16[128,128]{1,0:T(8,128)(2,1)} %weight_ref.3) | copy-start | bytes 98308
  65.4 27.6 %copy-start.4 = (f32[128]{0:T(128)S(1)}, f32[128]{0:T(128)}, u32[]{:S(2)}) copy-start(f32[128]{0:T(128)} %gain_ref.1) | copy-start | bytes 1540
  65.5 27.6 %copy-start.5 = (f32[128]{0:T(128)S(1)}, f32[128]{0:T(128)}, u32[]{:S(2)}) copy-start(f32[128]{0:T(128)} %bias_ref.1) | copy-start | bytes 1540

commit v3 on v2

--- a/solution.py
+++ b/solution.py
@@ -9,6 +9,7 @@
 BF16 = jnp.bfloat16
 EPS = 1e-05
 VMEM_LIMIT = 48 * 1024 * 1024
+PRODUCT_LIMIT = 24 * 1024 * 1024
 PROJECT_LIMIT = 60 * 1024 * 1024
 
 TILE_I = 256
@@ -20,8 +21,8 @@
 
 
 def layer_norm(x, gain, bias):
-    centre = jnp.mean(x, axis=-1, keepdims=True)
-    shifted = x - centre
+    share = jnp.full((CH, CH), 1.0 / CH, BF16)
+    shifted = x.astype(F32) - jnp.dot(x, share, preferred_element_type=F32)
     spread = jnp.mean(shifted * shifted, axis=-1, keepdims=True)
     return shifted * lax.rsqrt(spread + EPS) * gain + bias
 
@@ -41,7 +42,7 @@
     flat_staged = staged.reshape(2 * 2 * GROUP * PITCH, 128)
     batch = 64
     for part in range(TILE_I // batch):
-        x = pair_ref[part * batch : (part + 1) * batch].astype(F32).reshape(batch * KB, CH)
+        x = pair_ref[part * batch : (part + 1) * batch].reshape(batch * KB, CH)
         n = layer_norm(x, gain, bias)
         normed[part * batch : (part + 1) * batch, :KB, :] = n.reshape(batch, KB, CH)
     for k in range(KB):
@@ -90,7 +91,7 @@
 
 def gating_kernel(own_ref, pair_ref, gain_ref, bias_ref, weight_ref, out_ref, normed):
     batch, cols, _ = pair_ref.shape
-    x = pair_ref[...].astype(F32).reshape(batch * cols, CH)
+    x = pair_ref[...].reshape(batch * cols, CH)
     n = layer_norm(x, gain_ref[...], bias_ref[...])
     normed[:, :cols, :] = n.reshape(batch, cols, CH)
     flat = normed.reshape(batch * PITCH, CH)
@@ -126,37 +127,35 @@
     )(own, pair, gain, bias, weight)
 
 
-def product_kernel(core_ref, left_ref, right_ref, other_ref, out_ref):
-    core = core_ref[0]
-    for which in range(2):
-        block = (right_ref, other_ref)[which]
-        right = block[...].reshape(1024, TILE_I)
-        slot = core if which == 0 else 1 - core
-        for z in range(2):
-            left = left_ref[z].reshape(1024, TILE_I)
-            out_ref[z, 0, slot] = lax.dot_general(
-                right, left, (((0,), (0,)), ((), ())), preferred_element_type=F32
-            ).astype(BF16)
-
-
-def product(core, moved, other):
+def product_kernel(slot_ref, left_ref, right_ref, *refs):
+    out_ref = refs[-1]
+    right = right_ref[...].reshape(1024, TILE_I)
+    for z in range(2):
+        left = left_ref[z].reshape(1024, TILE_I)
+        out_ref[z, 0, 0] = lax.dot_general(
+            right, left, (((0,), (0,)), ((), ())), preferred_element_type=F32
+        ).astype(BF16)
+
+
+def product(slot, moved, right, right_spec, earlier, name):
+    shape = (2, 2, 2, TILE_I, TILE_I)
     return pl.pallas_call(
         product_kernel,
         grid_spec=pltpu.PrefetchScalarGridSpec(
             num_scalar_prefetch=1,
             grid=(2,),
             in_specs=[
-                pl.BlockSpec((2, 16, 1, TILE_K, TILE_I), lambda s, core: (0, 0, 0, 0, 0)),
-                pl.BlockSpec((1, 16, 1, TILE_K, TILE_I), lambda s, core: (s, 0, 1, 0, 0)),
-                pl.BlockSpec((1, 16, TILE_K, TILE_I), lambda s, core: (s, 0, 0, 0)),
-            ],
-            out_specs=pl.BlockSpec((2, 1, 2, TILE_I, TILE_I), lambda s, core: (0, s, 0, 0, 0)),
-        ),
-        out_shape=jax.ShapeDtypeStruct((2, 2, 2, TILE_I, TILE_I), BF16),
-        compiler_params=pltpu.CompilerParams(vmem_limit_bytes=VMEM_LIMIT),
-        cost_estimate=pl.CostEstimate(flops=1 << 30, bytes_accessed=4 << 20, transcendentals=0),
-        name="product",
-    )(core, moved, moved, other)
+                pl.BlockSpec((2, 16, 1, TILE_K, TILE_I), lambda s, slot: (0, 0, 0, 0, 0)),
+                right_spec,
+            ] + [pl.BlockSpec(memory_space=pl.ANY)] * len(earlier),
+            out_specs=pl.BlockSpec((2, 1, 1, TILE_I, TILE_I), lambda s, slot: (0, s, slot[0], 0, 0)),
+        ),
+        out_shape=jax.ShapeDtypeStruct(shape, BF16),
+        input_output_aliases={3: 0} if earlier else {},
+        compiler_params=pltpu.CompilerParams(vmem_limit_bytes=PRODUCT_LIMIT),
+        cost_estimate=pl.CostEstimate(flops=1 << 29, bytes_accessed=3 << 20, transcendentals=0),
+        name=name,
+    )(slot, moved, right, *earlier)
 
 
 def finish_kernel(prod_ref, gate_ref, gain_ref, bias_ref, weight_ref, out_ref, hidden, result):
@@ -229,7 +228,11 @@
     moved = moved.reshape(2, 16, 2, TILE_K, TILE_I)
     other = lax.ppermute(moved[:, :, 1], "core", [(0, 1), (1, 0)])
     gates = gating(own, pair, gain, bias, out_gate)
-    prod = product(core, moved, other).reshape(CH, TILE_K // 4, TILE_I)
+    here = pl.BlockSpec((1, 16, 1, TILE_K, TILE_I), lambda s, slot: (s, 0, 1, 0, 0))
+    there = pl.BlockSpec((1, 16, TILE_K, TILE_I), lambda s, slot: (s, 0, 0, 0))
+    prod = product(core, moved, moved, here, (), "product_own")
+    prod = product(1 - core, moved, other, there, (prod,), "product_other")
+    prod = prod.reshape(CH, TILE_K // 4, TILE_I)
     prod = lax.all_to_all(prod, ("zl", "x", "y", "chan"), 0, 0, tiled=True)
     return finish(prod, gates, hid_gain, hid_bias, out_weight)
 

time: 98.1 us -> 96.1 us (0.980)
  waiting for transfers between devices: 26.1 us -> 24.1 us
    ppermute x1, waiting for transfers between devices: 2.5 us -> 0.68 us  [on_device(): other = lax.ppermute(moved[:, :, 1], 'core', [(0, 1), (1, 0)])]
    pallas_call x1, Pallas kernels: 9.57 us -> 8.32 us  [project(): pl.pallas_call(project_kernel, grid=(TILE_K // KB,), in_specs=[pl.BlockSp...]
    pallas_call x1 -> x2, Pallas kernels: 2.47 us -> 3.56 us  [product(): pl.pallas_call(product_kernel, grid_spec=pltpu.PrefetchScalarGridSpec(num...]
  transfers between devices with their start and end apart: 2 -> 2, of which waited for: 2 -> 2; matrix products, arithmetic and copies ran while one was open for 0% -> 0% of each run, Pallas kernels for 4% -> 6%
where the time goes in v3:
time: 96.1 us; the launch traced here: 94.4 us
  blocking collectives  35.4 us (37%)
  waiting for transfers between devices  24.1 us (25%)
  Pallas kernels  19.3 us (20%)
  starting transfers between devices  14.3 us (15%)
  local copies, waits for them, and re-layouts  1.2 us (1%)
    all_to_all x1, blocking collectives, on_device(): moved = lax.all_to_all(sides, ('zl', 'x', 'y'), 0, 0, tiled=True)  35.4 us
    all_to_all x1, waiting for transfers between devices, on_device(): prod = lax.all_to_all(prod, ('zl', 'x', 'y', 'chan'), 0, 0, tiled=True)  23.5 us
    all_to_all x1, starting transfers between devices, on_device(): prod = lax.all_to_all(prod, ('zl', 'x', 'y', 'chan'), 0, 0, tiled=True)  11.8 us
    pallas_call x1, Pallas kernels, project(): pl.pallas_call(project_kernel, grid=(TILE_K // KB,), in_specs=[pl.BlockSp...  8.32 us
    pallas_call x1, Pallas kernels, gating(): pl.pallas_call(gating_kernel, grid_spec=pltpu.PrefetchScalarGridSpec(num_...  4.08 us
    pallas_call x2, Pallas kernels, product(): pl.pallas_call(product_kernel, grid_spec=pltpu.PrefetchScalarGridSpec(num...  3.56 us
    pallas_call x1, Pallas kernels, finish(): pl.pallas_call(finish_kernel, grid=(TILE_I // lanes,), in_specs=[pl.Block...  3.31 us
    ppermute x1, starting transfers between devices, on_device(): other = lax.ppermute(moved[:, :, 1], 'core', [(0, 1), (1, 0)])  2.53 us
  transfers between devices with their start and end apart: 2, of which 2 were waited for; matrix products, arithmetic and copies ran while one was open for 0% of the time, Pallas kernels for 6%

profile of v3, /device:TPU:1, one launch (start us, length us, event | category | flops | bytes accessed | tf_op | source)
XLA Modules:
  0.0 94.4 jit_solution(4448951462820842325)
XLA Ops:
  0.0 8.3 %project.1 = bf16[32,2,64,256]{3,2,1,0:T(8,128)(2,1)} custom-call(bf16[256,64,128]{2,1,0:T(8,128)(2,1)} %pair_ref.3, s32[64,256]{1,0:T(8,128)} %bitcast.22, f32[1,128]{1,0:T(1,128)} %bitcast.17, f32[1,128]{1,0:T(1,128)} %bitcast.19, bf16[32,128]{1,0:T(8,128)(2,1)} %bitcast.23, bf16[32,128]{1,0:T(8,128)(2,1)} %bitcast.24, bf16[32,128]{1,0:T(8,128)(2,1)} %bitcast.25, ...), custom_call_target="tpu_custom_call" | custom-call | flops 536870912 | bytes 7340032 | tf_op jit(solution)/shard_map/project/pallas_call | solution.py:65
  8.3 35.4 %all_to_all.10 = bf16[32,2,64,256]{3,2,1,0:T(8,128)(2,1)S(1)} all-to-all(bf16[32,2,64,256]{3,2,1,0:T(8,128)(2,1)} %project.1), channel_id=1, replica_groups=mesh['zl'=2,'core'=2,'x'=4,'y'=4,'chan'=4] {'zl','x','y'}, dimensions={0} | all-to-all | bytes 4194304 | tf_op jit(solution)/shard_map/all_to_all | solution.py:227
  43.7 0.1 copy.14
  43.8 1.0 %slice_bitcast_fusion = bf16[2,16,64,256]{3,2,1,0:T(8,128)(2,1)} fusion(bf16[2,16,2,64,256]{4,3,1,0,2:T(8,128)(2,1)S(1)} %bitcast.21), kind=kLoop, calls=%fused_computation | loop fusion | bytes 2097152 | tf_op jit(solution)/shard_map/squeeze | solution.py:229
  44.9 2.5 %collective-permute-start = (bf16[2,16,64,256]{3,2,1,0:T(8,128)(2,1)}, bf16[2,16,64,256]{3,2,1,0:T(8,128)(2,1)S(1)}, u32[]{:S(2)}, u32[]{:S(2)}) collective-permute-start(bf16[2,16,64,256]{3,2,1,0:T(8,128)(2,1)} %slice_bitcast_fusion), channel_id=1, source_target_pairs={{0,64},{64,0},{1,65},{65,1},{2,66},{66,2},{3,67},{67,3},{4,68},{68... | collective-permute-start | bytes 3145736 | tf_op jit(solution)/shard_map/ppermute | solution.py:229
  47.4 1.8 %product_own.1.refs_0_ = bf16[2,2,2,256,256]{4,3,2,1,0:T(8,128)(2,1)} custom-call(s32[1]{0:T(128)} %bitcast.slot_ref, bf16[2,16,2,64,256]{4,3,2,1,0:T(8,128)(2,1)S(1)} %bitcast.14, bf16[2,16,2,64,256]{4,3,2,1,0:T(8,128)(2,1)S(1)} %bitcast.15), custom_call_target="tpu_custom_call" | custom-call | flops 536870912 | bytes 3145728 | tf_op jit(solution)/shard_map/product_own/pallas_call | solution.py:142
  49.2 0.7 collective-permute-done.right_ref
  49.9 1.7 %product_other.1 = bf16[2,2,2,256,256]{4,3,2,1,0:T(8,128)(2,1)} custom-call(s32[1]{0:T(128)S(6)} %sub.3.slot_ref, bf16[2,16,2,64,256]{4,3,2,1,0:T(8,128)(2,1)S(1)} %bitcast.16, bf16[2,16,64,256]{3,2,1,0:T(8,128)(2,1)S(1)} %collective-permute-done.right_ref, bf16[2,2,2,256,256]{4,3,2,1,0:T(8,128)(2,1)} %product_own.1.refs_0_), custom_call_target="tpu_custom_call", output_to_operand_aliasing={{}: (3, {})} | custom-call | flops 536870912 | bytes 3145728 | tf_op jit(solution)/shard_map/product_other/pallas_call | solution.py:142
  51.6 0.0 copy-start
  51.7 0.0 copy-start.2
  51.7 0.0 copy-start.3
  51.7 11.8 %all-to-all-start.1 = ((bf16[128,16,256]{2,1,0:T(8,128)(2,1)}), bf16[128,16,256]{2,1,0:T(8,128)(2,1)S(1)}, u32[]{:S(2)}, u32[]{:S(2)}) async-start(bf16[128,16,256]{2,1,0:T(8,128)(2,1)} %bitcast.11), calls=%async_computation.1 | async-start | bytes 2097152 | tf_op jit(solution)/shard_map/all_to_all | solution.py:236
  63.4 0.0 copy-done
  63.5 0.0 copy-done.2
  63.5 0.0 copy-done.3
  63.5 0.0 copy-start.1
  63.5 0.0 copy-start.4
  63.5 0.0 copy-start.5
  63.5 4.1 %gating.1.gate_ref = f32[16,256,128]{2,1,0:T(8,128)S(1)} custom-call(s32[1]{0:T(128)} %bitcast.12.own_ref, bf16[256,64,128]{2,1,0:T(8,128)(2,1)} %pair_ref.3, f32[1,128]{1,0:T(1,128)S(1)} %bitcast.18, f32[1,128]{1,0:T(1,128)S(1)} %bitcast.20, bf16[128,128]{1,0:T(8,128)(2,1)S(1)} %copy-done), custom_call_target="tpu_custom_call" | custom-call | flops 134217728 | bytes 3145728 | tf_op jit(solution)/shard_map/gating/pallas_call | solution.py:107
  67.6 23.5 %all-to-all-done.1.prod_ref = bf16[128,16,256]{2,1,0:T(8,128)(2,1)S(1)} async-done(((bf16[128,16,256]{2,1,0:T(8,128)(2,1)}), bf16[128,16,256]{2,1,0:T(8,128)(2,1)S(1)}, u32[]{:S(2)}, u32[]{:S(2)}) %all-to-all-start.1) | async-done | bytes 1048608 | tf_op jit(solution)/shard_map/all_to_all | solution.py:236
  91.1 0.0 copy-done.1
  91.1 0.0 copy-done.4
  91.1 0.0 copy-done.5
  91.1 3.3 %finish.1 = bf16[256,16,128]{2,1,0:T(8,128)(2,1)} custom-call(bf16[128,16,256]{2,1,0:T(8,128)(2,1)S(1)} %all-to-all-done.1.prod_ref, f32[16,256,128]{2,1,0:T(8,128)S(1)} %gating.1.gate_ref, f32[128]{0:T(128)S(1)} %copy-done.4, f32[128]{0:T(128)S(1)} %copy-done.5, bf16[128,128]{1,0:T(8,128)(2,1)S(1)} %copy-done.1), custom_call_target="tpu_custom_call" | custom-call | flops 134217728 | bytes 4194304 | tf_op jit(solution)/shard_map/finish/pallas_call | solution.py:192
Async XLA Ops:
  44.9 5.0 %collective-permute-start = (bf16[2,16,64,256]{3,2,1,0:T(8,128)(2,1)}, bf16[2,16,64,256]{3,2,1,0:T(8,128)(2,1)S(1)}, u32[]{:S(2)}, u32[]{:S(2)}) collective-permute-start(bf16[2,16,64,256]{3,2,1,0:T(8,128)(2,1)} %slice_bitcast_fusion), channel_id=1, source_target_pairs={{0,64},{64,0},{1,65},{65,1},{2,66},{66,2},{3,67},{67,3},{4,68},{68... | collective-permute-start | bytes 3145736 | tf_op jit(solution)/shard_map/ppermute | solution.py:229
  51.6 11.8 %copy-start = (bf16[128,128]{1,0:T(8,128)(2,1)S(1)}, bf16[128,128]{1,0:T(8,128)(2,1)}, u32[]{:S(2)}) copy-start(bf16[128,128]{1,0:T(8,128)(2,1)} %weight_ref.2) | copy-start | bytes 98308
  51.7 11.8 %copy-start.2 = (f32[128]{0:T(128)S(1)}, f32[128]{0:T(128)}, u32[]{:S(2)}) copy-start(f32[128]{0:T(128)} %param.14) | copy-start | bytes 1540
  51.7 11.8 %copy-start.3 = (f32[128]{0:T(128)S(1)}, f32[128]{0:T(128)}, u32[]{:S(2)}) copy-start(f32[128]{0:T(128)} %param.15) | copy-start | bytes 1540
  51.7 39.4 %all-to-all-start.1 = ((bf16[128,16,256]{2,1,0:T(8,128)(2,1)}), bf16[128,16,256]{2,1,0:T(8,128)(2,1)S(1)}, u32[]{:S(2)}, u32[]{:S(2)}) async-start(bf16[128,16,256]{2,1,0:T(8,128)(2,1)} %bitcast.11), calls=%async_computation.1 | async-start | bytes 2097152 | tf_op jit(solution)/shard_map/all_to_all | solution.py:236
  63.5 27.6 %copy-start.1 = (bf16[128,128]{1,0:T(8,128)(2,1)S(1)}, bf16[128,128]{1,0:T(8,128)(2,1)}, u32[]{:S(2)}) copy-start(bf16[128,128]{1,0:T(8,128)(2,1)} %weight_ref.3) | copy-start | bytes 98308
  63.5 27.6 %copy-start.4 = (f32[128]{0:T(128)S(1)}, f32[128]{0:T(128)}, u32[]{:S(2)}) copy-start(f32[128]{0:T(128)} %gain_ref.1) | copy-start | bytes 1540
  63.5 27.6 %copy-start.5 = (f32[128]{0:T(128)S(1)}, f32[128]{0:T(128)}, u32[]{:S(2)}) copy-start(f32[128]{0:T(128)} %bias_ref.1) | copy-start | bytes 1540

commit v4 on v3

--- a/solution.py
+++ b/solution.py
@@ -119,7 +119,7 @@
             scratch_shapes=[pltpu.VMEM((batch, PITCH, CH), F32)],
         ),
         out_shape=jax.ShapeDtypeStruct((cols, TILE_I, CH), F32),
-        compiler_params=pltpu.CompilerParams(vmem_limit_bytes=VMEM_LIMIT),
+        compiler_params=pltpu.CompilerParams(vmem_limit_bytes=PROJECT_LIMIT),
         cost_estimate=pl.CostEstimate(
             flops=2 * TILE_I * cols * CH * CH, bytes_accessed=3 << 20, transcendentals=1 << 19
         ),
@@ -163,12 +163,11 @@
     lanes = prod_ref.shape[2]
     batch = 8
 
-    def add(part, sums):
-        x = prod_ref[pl.ds(part * batch, batch)].astype(F32)
-        return sums[0] + jnp.sum(x, axis=0), sums[1] + jnp.sum(x * x, axis=0)
-
-    zero = jnp.zeros((cols, lanes), F32)
-    first, second = lax.fori_loop(0, CH // batch, add, (zero, zero))
+    first = jnp.zeros((cols, lanes), F32)
+    second = jnp.zeros((cols, lanes), F32)
+    for part in range(CH // batch):
+        x = prod_ref[part * batch : (part + 1) * batch].astype(F32)
+        first, second = first + jnp.sum(x, axis=0), second + jnp.sum(x * x, axis=0)
     mean = first * (1.0 / CH)
     scale = lax.rsqrt(second * (1.0 / CH) - mean * mean + EPS)
     flat_hidden = hidden.reshape(CH * PITCH, lanes)
@@ -225,9 +224,10 @@
         pair, pair_mask.T, gain, bias, left_value.T, left_gate.T, right_value.T, right_gate.T
     )
     moved = lax.all_to_all(sides, ("zl", "x", "y"), 0, 0, tiled=True)
+    gates = gating(own, pair, gain, bias, out_gate)
+    moved, gates = lax.optimization_barrier((moved, gates))
     moved = moved.reshape(2, 16, 2, TILE_K, TILE_I)
     other = lax.ppermute(moved[:, :, 1], "core", [(0, 1), (1, 0)])
-    gates = gating(own, pair, gain, bias, out_gate)
     here = pl.BlockSpec((1, 16, 1, TILE_K, TILE_I), lambda s, slot: (s, 0, 1, 0, 0))
     there = pl.BlockSpec((1, 16, TILE_K, TILE_I), lambda s, slot: (s, 0, 0, 0))
     prod = product(core, moved, moved, here, (), "product_own")

time: 96.1 us -> 95.8 us (level)
  blocking collectives: 35.4 us -> 39.1 us
  waiting for transfers between devices: 24.1 us -> 21.8 us
  starting transfers between devices: 14.3 us -> 13.2 us
    all_to_all x1, blocking collectives: 35.4 us -> 39.1 us  [on_device(): prod = lax.all_to_all(prod, ('zl', 'x', 'y', 'chan'), 0, 0, tiled=True)]
    all_to_all x1, waiting for transfers between devices: 23.5 us -> 20.5 us  [on_device(): moved = lax.all_to_all(sides, ('zl', 'x', 'y'), 0, 0, tiled=True)]
    all_to_all x1, starting transfers between devices: 11.8 us -> 9.22 us  [on_device(): moved = lax.all_to_all(sides, ('zl', 'x', 'y'), 0, 0, tiled=True)]
    ppermute x1, starting transfers between devices: 2.53 us -> 3.98 us  [on_device(): other = lax.ppermute(moved[:, :, 1], 'core', [(0, 1), (1, 0)])]
    pallas_call x2, Pallas kernels: 3.56 us -> 2.2 us  [product(): pl.pallas_call(product_kernel, grid_spec=pltpu.PrefetchScalarGridSpec(num...]
    pallas_call x1, Pallas kernels: 4.08 us -> 5.06 us  [gating(): pl.pallas_call(gating_kernel, grid_spec=pltpu.PrefetchScalarGridSpec(num_...]
  transfers between devices with their start and end apart: 2 -> 2, of which waited for: 2 -> 2; matrix products, arithmetic and copies ran while one was open for 0% -> 0% of each run, Pallas kernels for 6% -> 7%
where the time goes in v4:
time: 95.8 us; the launch traced here: 94.1 us
  blocking collectives  39.1 us (41%)
  waiting for transfers between devices  21.8 us (23%)
  Pallas kernels  18.7 us (20%)
  starting transfers between devices  13.2 us (14%)
  local copies, waits for them, and re-layouts  1.2 us (1%)
    all_to_all x1, blocking collectives, on_device(): prod = lax.all_to_all(prod, ('zl', 'x', 'y', 'chan'), 0, 0, tiled=True)  39.1 us
    all_to_all x1, waiting for transfers between devices, on_device(): moved = lax.all_to_all(sides, ('zl', 'x', 'y'), 0, 0, tiled=True)  20.5 us
    all_to_all x1, starting transfers between devices, on_device(): moved = lax.all_to_all(sides, ('zl', 'x', 'y'), 0, 0, tiled=True)  9.22 us
    pallas_call x1, Pallas kernels, project(): pl.pallas_call(project_kernel, grid=(TILE_K // KB,), in_specs=[pl.BlockSp...  8.32 us
    pallas_call x1, Pallas kernels, gating(): pl.pallas_call(gating_kernel, grid_spec=pltpu.PrefetchScalarGridSpec(num_...  5.06 us
    ppermute x1, starting transfers between devices, on_device(): other = lax.ppermute(moved[:, :, 1], 'core', [(0, 1), (1, 0)])  3.98 us
    pallas_call x1, Pallas kernels, finish(): pl.pallas_call(finish_kernel, grid=(TILE_I // lanes,), in_specs=[pl.Block...  3.13 us
    pallas_call x2, Pallas kernels, product(): pl.pallas_call(product_kernel, grid_spec=pltpu.PrefetchScalarGridSpec(num...  2.2 us
  transfers between devices with their start and end apart: 2, of which 2 were waited for; matrix products, arithmetic and copies ran while one was open for 0% of the time, Pallas kernels for 7%

profile of v4, /device:TPU:1, one launch (start us, length us, event | category | flops | bytes accessed | tf_op | source)
XLA Modules:
  0.0 94.1 jit_solution(16838252099986355890)
XLA Ops:
  0.0 8.3 %project.1 = bf16[32,2,64,256]{3,2,1,0:T(8,128)(2,1)} custom-call(bf16[256,64,128]{2,1,0:T(8,128)(2,1)} %pair_ref.3, s32[64,256]{1,0:T(8,128)} %bitcast.19, f32[1,128]{1,0:T(1,128)} %bitcast.24, f32[1,128]{1,0:T(1,128)} %bitcast.26, bf16[32,128]{1,0:T(8,128)(2,1)} %bitcast.20, bf16[32,128]{1,0:T(8,128)(2,1)} %bitcast.21, bf16[32,128]{1,0:T(8,128)(2,1)} %bitcast.22, ...), custom_call_target="tpu_custom_call" | custom-call | flops 536870912 | bytes 7340032 | tf_op jit(solution)/shard_map/project/pallas_call | solution.py:65
  8.3 9.2 %all-to-all-start = ((bf16[32,2,64,256]{3,2,1,0:T(8,128)(2,1)}), bf16[32,2,64,256]{3,2,1,0:T(8,128)(2,1)S(1)}, u32[]{:S(2)}, u32[]{:S(2)}) async-start(bf16[32,2,64,256]{3,2,1,0:T(8,128)(2,1)} %project.1), calls=%async_computation | async-start | bytes 4194304 | tf_op jit(solution)/shard_map/all_to_all | solution.py:226
  17.6 5.1 %gating.1.gate_ref = f32[16,256,128]{2,1,0:T(8,128)} custom-call(s32[1]{0:T(128)} %bitcast.8.own_ref, bf16[256,64,128]{2,1,0:T(8,128)(2,1)} %pair_ref.3, f32[1,128]{1,0:T(1,128)} %bitcast.25, f32[1,128]{1,0:T(1,128)} %bitcast.27, bf16[128,128]{1,0:T(8,128)(2,1)} %weight_ref.2), custom_call_target="tpu_custom_call" | custom-call | flops 134217728 | bytes 3145728 | tf_op jit(solution)/shard_map/gating/pallas_call | solution.py:107
  22.6 20.5 %all-to-all-done = bf16[32,2,64,256]{3,2,1,0:T(8,128)(2,1)S(1)} async-done(((bf16[32,2,64,256]{3,2,1,0:T(8,128)(2,1)}), bf16[32,2,64,256]{3,2,1,0:T(8,128)(2,1)S(1)}, u32[]{:S(2)}, u32[]{:S(2)}) %all-to-all-start) | async-done | bytes 2097184 | tf_op jit(solution)/shard_map/all_to_all | solution.py:226
  43.1 0.1 copy.14
  43.2 1.0 %slice_bitcast_fusion = bf16[2,16,64,256]{3,2,1,0:T(8,128)(2,1)} fusion(bf16[2,16,2,64,256]{4,3,1,0,2:T(8,128)(2,1)S(1)} %bitcast.18), kind=kLoop, calls=%fused_computation | loop fusion | bytes 2097152 | tf_op jit(solution)/shard_map/squeeze | solution.py:230
  44.3 4.0 %collective-permute-start = (bf16[2,16,64,256]{3,2,1,0:T(8,128)(2,1)}, bf16[2,16,64,256]{3,2,1,0:T(8,128)(2,1)S(1)}, u32[]{:S(2)}, u32[]{:S(2)}) collective-permute-start(bf16[2,16,64,256]{3,2,1,0:T(8,128)(2,1)} %slice_bitcast_fusion), channel_id=1, source_target_pairs={{0,64},{64,0},{1,65},{65,1},{2,66},{66,2},{3,67},{67,3},{4,68},{68... | collective-permute-start | bytes 3145736 | tf_op jit(solution)/shard_map/ppermute | solution.py:230
  48.3 1.1 %product_own.1.refs_0_ = bf16[2,2,2,256,256]{4,3,2,1,0:T(8,128)(2,1)S(1)} custom-call(s32[1]{0:T(128)} %bitcast.slot_ref, bf16[2,16,2,64,256]{4,3,2,1,0:T(8,128)(2,1)S(1)} %bitcast.14, bf16[2,16,2,64,256]{4,3,2,1,0:T(8,128)(2,1)S(1)} %bitcast.15), custom_call_target="tpu_custom_call" | custom-call | flops 536870912 | bytes 3145728 | tf_op jit(solution)/shard_map/product_own/pallas_call | solution.py:142
  49.4 1.3 %collective-permute-done.right_ref = bf16[2,16,64,256]{3,2,1,0:T(8,128)(2,1)S(1)} collective-permute-done((bf16[2,16,64,256]{3,2,1,0:T(8,128)(2,1)}, bf16[2,16,64,256]{3,2,1,0:T(8,128)(2,1)S(1)}, u32[]{:S(2)}, u32[]{:S(2)}) %collective-permute-start) | collective-permute-done | bytes 1048608 | tf_op jit(solution)/shard_map/ppermute | solution.py:230
  50.8 0.0 copy-start.1
  50.8 1.1 %product_other.1 = bf16[2,2,2,256,256]{4,3,2,1,0:T(8,128)(2,1)S(1)} custom-call(s32[1]{0:T(128)S(6)} %sub.3.slot_ref, bf16[2,16,2,64,256]{4,3,2,1,0:T(8,128)(2,1)S(1)} %bitcast.16, bf16[2,16,64,256]{3,2,1,0:T(8,128)(2,1)S(1)} %collective-permute-done.right_ref, bf16[2,2,2,256,256]{4,3,2,1,0:T(8,128)(2,1)S(1)} %product_own.1.refs_0_), custom_call_target="tpu_custom_call", output_to_operand_aliasing={{}: (3, {})} | custom-call | flops 536870912 | bytes 3145728 | tf_op jit(solution)/shard_map/product_other/pallas_call | solution.py:142
  51.8 0.0 copy-start
  51.8 0.0 copy-start.2
  51.8 0.0 copy-start.3
  51.9 39.1 %all_to_all.10.prod_ref = bf16[128,16,256]{2,1,0:T(8,128)(2,1)S(1)} all-to-all(bf16[128,16,256]{2,1,0:T(8,128)(2,1)S(1)} %bitcast.17), channel_id=1, replica_groups=mesh['zl'=2,'core'=2,'x'=4,'y'=4,'chan'=4] {'zl','x','y','chan'}, dimensions={0} | all-to-all | bytes 2097152 | tf_op jit(solution)/shard_map/all_to_all | solution.py:236
  91.0 0.0 copy-done.1
  91.0 0.0 copy-done
  91.0 0.0 copy-done.2
  91.0 0.0 copy-done.3
  91.0 3.1 %finish.1 = bf16[256,16,128]{2,1,0:T(8,128)(2,1)} custom-call(bf16[128,16,256]{2,1,0:T(8,128)(2,1)S(1)} %all_to_all.10.prod_ref, f32[16,256,128]{2,1,0:T(8,128)S(1)} %copy-done, f32[128]{0:T(128)S(1)} %copy-done.2, f32[128]{0:T(128)S(1)} %copy-done.3, bf16[128,128]{1,0:T(8,128)(2,1)S(1)} %copy-done.1), custom_call_target="tpu_custom_call" | custom-call | flops 134217728 | bytes 4194304 | tf_op jit(solution)/shard_map/finish/pallas_call | solution.py:191
Async XLA Ops:
  8.3 34.8 %all-to-all-start = ((bf16[32,2,64,256]{3,2,1,0:T(8,128)(2,1)}), bf16[32,2,64,256]{3,2,1,0:T(8,128)(2,1)S(1)}, u32[]{:S(2)}, u32[]{:S(2)}) async-start(bf16[32,2,64,256]{3,2,1,0:T(8,128)(2,1)} %project.1), calls=%async_computation | async-start | bytes 4194304 | tf_op jit(solution)/shard_map/all_to_all | solution.py:226
  44.3 6.5 %collective-permute-start = (bf16[2,16,64,256]{3,2,1,0:T(8,128)(2,1)}, bf16[2,16,64,256]{3,2,1,0:T(8,128)(2,1)S(1)}, u32[]{:S(2)}, u32[]{:S(2)}) collective-permute-start(bf16[2,16,64,256]{3,2,1,0:T(8,128)(2,1)} %slice_bitcast_fusion), channel_id=1, source_target_pairs={{0,64},{64,0},{1,65},{65,1},{2,66},{66,2},{3,67},{67,3},{4,68},{68... | collective-permute-start | bytes 3145736 | tf_op jit(solution)/shard_map/ppermute | solution.py:230
  50.8 40.2 %copy-start.1 = (bf16[128,128]{1,0:T(8,128)(2,1)S(1)}, bf16[128,128]{1,0:T(8,128)(2,1)}, u32[]{:S(2)}) copy-start(bf16[128,128]{1,0:T(8,128)(2,1)} %weight_ref.3) | copy-start | bytes 98308
  51.8 39.2 %copy-start = (f32[16,256,128]{2,1,0:T(8,128)S(1)}, f32[16,256,128]{2,1,0:T(8,128)}, u32[]{:S(2)}) copy-start(f32[16,256,128]{2,1,0:T(8,128)} %gating.1.gate_ref) | copy-start | bytes 6291460
  51.8 39.2 %copy-start.2 = (f32[128]{0:T(128)S(1)}, f32[128]{0:T(128)}, u32[]{:S(2)}) copy-start(f32[128]{0:T(128)} %gain_ref.1) | copy-start | bytes 1540
  51.8 39.2 %copy-start.3 = (f32[128]{0:T(128)S(1)}, f32[128]{0:T(128)}, u32[]{:S(2)}) copy-start(f32[128]{0:T(128)} %bias_ref.1) | copy-start | bytes 1540

commit v5 on v4

--- a/solution.py
+++ b/solution.py
@@ -119,7 +119,7 @@
             scratch_shapes=[pltpu.VMEM((batch, PITCH, CH), F32)],
         ),
         out_shape=jax.ShapeDtypeStruct((cols, TILE_I, CH), F32),
-        compiler_params=pltpu.CompilerParams(vmem_limit_bytes=PROJECT_LIMIT),
+        compiler_params=pltpu.CompilerParams(vmem_limit_bytes=VMEM_LIMIT),
         cost_estimate=pl.CostEstimate(
             flops=2 * TILE_I * cols * CH * CH, bytes_accessed=3 << 20, transcendentals=1 << 19
         ),
@@ -224,10 +224,9 @@
         pair, pair_mask.T, gain, bias, left_value.T, left_gate.T, right_value.T, right_gate.T
     )
     moved = lax.all_to_all(sides, ("zl", "x", "y"), 0, 0, tiled=True)
-    gates = gating(own, pair, gain, bias, out_gate)
-    moved, gates = lax.optimization_barrier((moved, gates))
     moved = moved.reshape(2, 16, 2, TILE_K, TILE_I)
     other = lax.ppermute(moved[:, :, 1], "core", [(0, 1), (1, 0)])
+    gates = gating(own, pair, gain, bias, out_gate)
     here = pl.BlockSpec((1, 16, 1, TILE_K, TILE_I), lambda s, slot: (s, 0, 1, 0, 0))
     there = pl.BlockSpec((1, 16, TILE_K, TILE_I), lambda s, slot: (s, 0, 0, 0))
     prod = product(core, moved, moved, here, (), "product_own")

time: 95.8 us -> 95.9 us (level)
  blocking collectives: 39.1 us -> 35.4 us
  waiting for transfers between devices: 21.8 us -> 24.1 us
  starting transfers between devices: 13.2 us -> 14.3 us
    all_to_all x1, blocking collectives: 39.1 us -> 35.4 us  [on_device(): moved = lax.all_to_all(sides, ('zl', 'x', 'y'), 0, 0, tiled=True)]
    all_to_all x1, waiting for transfers between devices: 20.5 us -> 23.5 us  [on_device(): prod = lax.all_to_all(prod, ('zl', 'x', 'y', 'chan'), 0, 0, tiled=True)]
    all_to_all x1, starting transfers between devices: 9.22 us -> 11.8 us  [on_device(): prod = lax.all_to_all(prod, ('zl', 'x', 'y', 'chan'), 0, 0, tiled=True)]
    ppermute x1, starting transfers between devices: 3.98 us -> 2.53 us  [on_device(): other = lax.ppermute(moved[:, :, 1], 'core', [(0, 1), (1, 0)])]
    pallas_call x2, Pallas kernels: 2.2 us -> 3.56 us  [product(): pl.pallas_call(product_kernel, grid_spec=pltpu.PrefetchScalarGridSpec(num...]
    pallas_call x1, Pallas kernels: 5.06 us -> 4.08 us  [gating(): pl.pallas_call(gating_kernel, grid_spec=pltpu.PrefetchScalarGridSpec(num_...]
  transfers between devices with their start and end apart: 2 -> 2, of which waited for: 2 -> 2; matrix products, arithmetic and copies ran while one was open for 0% -> 0% of each run, Pallas kernels for 7% -> 6%
where the time goes in v5:
time: 95.9 us; the launch traced here: 94.2 us
  blocking collectives  35.4 us (37%)
  waiting for transfers between devices  24.1 us (25%)
  Pallas kernels  19.1 us (20%)
  starting transfers between devices  14.3 us (15%)
  local copies, waits for them, and re-layouts  1.2 us (1%)
    all_to_all x1, blocking collectives, on_device(): moved = lax.all_to_all(sides, ('zl', 'x', 'y'), 0, 0, tiled=True)  35.4 us
    all_to_all x1, waiting for transfers between devices, on_device(): prod = lax.all_to_all(prod, ('zl', 'x', 'y', 'chan'), 0, 0, tiled=True)  23.5 us
    all_to_all x1, starting transfers between devices, on_device(): prod = lax.all_to_all(prod, ('zl', 'x', 'y', 'chan'), 0, 0, tiled=True)  11.8 us
    pallas_call x1, Pallas kernels, project(): pl.pallas_call(project_kernel, grid=(TILE_K // KB,), in_specs=[pl.BlockSp...  8.32 us
    pallas_call x1, Pallas kernels, gating(): pl.pallas_call(gating_kernel, grid_spec=pltpu.PrefetchScalarGridSpec(num_...  4.08 us
    pallas_call x2, Pallas kernels, product(): pl.pallas_call(product_kernel, grid_spec=pltpu.PrefetchScalarGridSpec(num...  3.56 us
    pallas_call x1, Pallas kernels, finish(): pl.pallas_call(finish_kernel, grid=(TILE_I // lanes,), in_specs=[pl.Block...  3.13 us
    ppermute x1, starting transfers between devices, on_device(): other = lax.ppermute(moved[:, :, 1], 'core', [(0, 1), (1, 0)])  2.53 us
  transfers between devices with their start and end apart: 2, of which 2 were waited for; matrix products, arithmetic and copies ran while one was open for 0% of the time, Pallas kernels for 6%

profile of v5, /device:TPU:1, one launch (start us, length us, event | category | flops | bytes accessed | tf_op | source)
XLA Modules:
  0.0 94.2 jit_solution(4402122874605973456)
XLA Ops:
  0.0 8.3 %project.1 = bf16[32,2,64,256]{3,2,1,0:T(8,128)(2,1)} custom-call(bf16[256,64,128]{2,1,0:T(8,128)(2,1)} %pair_ref.3, s32[64,256]{1,0:T(8,128)} %bitcast.22, f32[1,128]{1,0:T(1,128)} %bitcast.17, f32[1,128]{1,0:T(1,128)} %bitcast.19, bf16[32,128]{1,0:T(8,128)(2,1)} %bitcast.23, bf16[32,128]{1,0:T(8,128)(2,1)} %bitcast.24, bf16[32,128]{1,0:T(8,128)(2,1)} %bitcast.25, ...), custom_call_target="tpu_custom_call" | custom-call | flops 536870912 | bytes 7340032 | tf_op jit(solution)/shard_map/project/pallas_call | solution.py:65
  8.3 35.4 %all_to_all.10 = bf16[32,2,64,256]{3,2,1,0:T(8,128)(2,1)S(1)} all-to-all(bf16[32,2,64,256]{3,2,1,0:T(8,128)(2,1)} %project.1), channel_id=1, replica_groups=mesh['zl'=2,'core'=2,'x'=4,'y'=4,'chan'=4] {'zl','x','y'}, dimensions={0} | all-to-all | bytes 4194304 | tf_op jit(solution)/shard_map/all_to_all | solution.py:226
  43.7 0.1 copy.14
  43.8 1.0 %slice_bitcast_fusion = bf16[2,16,64,256]{3,2,1,0:T(8,128)(2,1)} fusion(bf16[2,16,2,64,256]{4,3,1,0,2:T(8,128)(2,1)S(1)} %bitcast.21), kind=kLoop, calls=%fused_computation | loop fusion | bytes 2097152 | tf_op jit(solution)/shard_map/squeeze | solution.py:228
  44.9 2.5 %collective-permute-start = (bf16[2,16,64,256]{3,2,1,0:T(8,128)(2,1)}, bf16[2,16,64,256]{3,2,1,0:T(8,128)(2,1)S(1)}, u32[]{:S(2)}, u32[]{:S(2)}) collective-permute-start(bf16[2,16,64,256]{3,2,1,0:T(8,128)(2,1)} %slice_bitcast_fusion), channel_id=1, source_target_pairs={{0,64},{64,0},{1,65},{65,1},{2,66},{66,2},{3,67},{67,3},{4,68},{68... | collective-permute-start | bytes 3145736 | tf_op jit(solution)/shard_map/ppermute | solution.py:228
  47.4 1.8 %product_own.1.refs_0_ = bf16[2,2,2,256,256]{4,3,2,1,0:T(8,128)(2,1)} custom-call(s32[1]{0:T(128)} %bitcast.slot_ref, bf16[2,16,2,64,256]{4,3,2,1,0:T(8,128)(2,1)S(1)} %bitcast.14, bf16[2,16,2,64,256]{4,3,2,1,0:T(8,128)(2,1)S(1)} %bitcast.15), custom_call_target="tpu_custom_call" | custom-call | flops 536870912 | bytes 3145728 | tf_op jit(solution)/shard_map/product_own/pallas_call | solution.py:142
  49.2 0.7 collective-permute-done.right_ref
  49.9 1.7 %product_other.1 = bf16[2,2,2,256,256]{4,3,2,1,0:T(8,128)(2,1)} custom-call(s32[1]{0:T(128)S(6)} %sub.3.slot_ref, bf16[2,16,2,64,256]{4,3,2,1,0:T(8,128)(2,1)S(1)} %bitcast.16, bf16[2,16,64,256]{3,2,1,0:T(8,128)(2,1)S(1)} %collective-permute-done.right_ref, bf16[2,2,2,256,256]{4,3,2,1,0:T(8,128)(2,1)} %product_own.1.refs_0_), custom_call_target="tpu_custom_call", output_to_operand_aliasing={{}: (3, {})} | custom-call | flops 536870912 | bytes 3145728 | tf_op jit(solution)/shard_map/product_other/pallas_call | solution.py:142
  51.6 0.0 copy-start
  51.7 0.0 copy-start.2
  51.7 0.0 copy-start.3
  51.7 11.8 %all-to-all-start.1 = ((bf16[128,16,256]{2,1,0:T(8,128)(2,1)}), bf16[128,16,256]{2,1,0:T(8,128)(2,1)S(1)}, u32[]{:S(2)}, u32[]{:S(2)}) async-start(bf16[128,16,256]{2,1,0:T(8,128)(2,1)} %bitcast.11), calls=%async_computation.1 | async-start | bytes 2097152 | tf_op jit(solution)/shard_map/all_to_all | solution.py:235
  63.4 0.0 copy-done
  63.5 0.0 copy-done.2
  63.5 0.0 copy-done.3
  63.5 0.0 copy-start.1
  63.5 0.0 copy-start.4
  63.5 0.0 copy-start.5
  63.5 4.1 %gating.1.gate_ref = f32[16,256,128]{2,1,0:T(8,128)S(1)} custom-call(s32[1]{0:T(128)} %bitcast.12.own_ref, bf16[256,64,128]{2,1,0:T(8,128)(2,1)} %pair_ref.3, f32[1,128]{1,0:T(1,128)S(1)} %bitcast.18, f32[1,128]{1,0:T(1,128)S(1)} %bitcast.20, bf16[128,128]{1,0:T(8,128)(2,1)S(1)} %copy-done), custom_call_target="tpu_custom_call" | custom-call | flops 134217728 | bytes 3145728 | tf_op jit(solution)/shard_map/gating/pallas_call | solution.py:107
  67.6 23.5 %all-to-all-done.1.prod_ref = bf16[128,16,256]{2,1,0:T(8,128)(2,1)S(1)} async-done(((bf16[128,16,256]{2,1,0:T(8,128)(2,1)}), bf16[128,16,256]{2,1,0:T(8,128)(2,1)S(1)}, u32[]{:S(2)}, u32[]{:S(2)}) %all-to-all-start.1) | async-done | bytes 1048608 | tf_op jit(solution)/shard_map/all_to_all | solution.py:235
  91.1 0.0 copy-done.1
  91.1 0.0 copy-done.4
  91.1 0.0 copy-done.5
  91.1 3.1 %finish.1 = bf16[256,16,128]{2,1,0:T(8,128)(2,1)} custom-call(bf16[128,16,256]{2,1,0:T(8,128)(2,1)S(1)} %all-to-all-done.1.prod_ref, f32[16,256,128]{2,1,0:T(8,128)S(1)} %gating.1.gate_ref, f32[128]{0:T(128)S(1)} %copy-done.4, f32[128]{0:T(128)S(1)} %copy-done.5, bf16[128,128]{1,0:T(8,128)(2,1)S(1)} %copy-done.1), custom_call_target="tpu_custom_call" | custom-call | flops 134217728 | bytes 4194304 | tf_op jit(solution)/shard_map/finish/pallas_call | solution.py:191
Async XLA Ops:
  44.9 5.0 %collective-permute-start = (bf16[2,16,64,256]{3,2,1,0:T(8,128)(2,1)}, bf16[2,16,64,256]{3,2,1,0:T(8,128)(2,1)S(1)}, u32[]{:S(2)}, u32[]{:S(2)}) collective-permute-start(bf16[2,16,64,256]{3,2,1,0:T(8,128)(2,1)} %slice_bitcast_fusion), channel_id=1, source_target_pairs={{0,64},{64,0},{1,65},{65,1},{2,66},{66,2},{3,67},{67,3},{4,68},{68... | collective-permute-start | bytes 3145736 | tf_op jit(solution)/shard_map/ppermute | solution.py:228
  51.6 11.8 %copy-start = (bf16[128,128]{1,0:T(8,128)(2,1)S(1)}, bf16[128,128]{1,0:T(8,128)(2,1)}, u32[]{:S(2)}) copy-start(bf16[128,128]{1,0:T(8,128)(2,1)} %weight_ref.2) | copy-start | bytes 98308
  51.7 11.8 %copy-start.2 = (f32[128]{0:T(128)S(1)}, f32[128]{0:T(128)}, u32[]{:S(2)}) copy-start(f32[128]{0:T(128)} %param.14) | copy-start | bytes 1540
  51.7 11.8 %copy-start.3 = (f32[128]{0:T(128)S(1)}, f32[128]{0:T(128)}, u32[]{:S(2)}) copy-start(f32[128]{0:T(128)} %param.15) | copy-start | bytes 1540
  51.7 39.4 %all-to-all-start.1 = ((bf16[128,16,256]{2,1,0:T(8,128)(2,1)}), bf16[128,16,256]{2,1,0:T(8,128)(2,1)S(1)}, u32[]{:S(2)}, u32[]{:S(2)}) async-start(bf16[128,16,256]{2,1,0:T(8,128)(2,1)} %bitcast.11), calls=%async_computation.1 | async-start | bytes 2097152 | tf_op jit(solution)/shard_map/all_to_all | solution.py:235
  63.5 27.6 %copy-start.1 = (bf16[128,128]{1,0:T(8,128)(2,1)S(1)}, bf16[128,128]{1,0:T(8,128)(2,1)}, u32[]{:S(2)}) copy-start(bf16[128,128]{1,0:T(8,128)(2,1)} %weight_ref.3) | copy-start | bytes 98308
  63.5 27.6 %copy-start.4 = (f32[128]{0:T(128)S(1)}, f32[128]{0:T(128)}, u32[]{:S(2)}) copy-start(f32[128]{0:T(128)} %gain_ref.1) | copy-start | bytes 1540
  63.5 27.6 %copy-start.5 = (f32[128]{0:T(128)S(1)}, f32[128]{0:T(128)}, u32[]{:S(2)}) copy-start(f32[128]{0:T(128)} %bias_ref.1) | copy-start | bytes 1540
